TPU v7x, 256 devices: a whole 4x4x8 slice. The times are simulated.
256 devices in a mesh: gx: 32 (over x, z_lo, core), gy: 8 (over z_hi, y).
Axes of the slice: x: 4, y: 4, z: 8 (z_hi: 2, z_lo: 4; z = z_hi * 4 + z_lo), core: 2. Of those that a mesh axis runs over, the one named last changes fastest.
Arguments:
- positions: bfloat16 [3, 32768], P(None, ('gx', 'gy')), as said below
- species: int32 [32768], P(('gx', 'gy')), may hold values from 0 to 9
- neighbours: int32 [32768, 48], P(('gx', 'gy')), may hold values from 0 to 511
- counts: int32 [32768], P(('gx', 'gy')), may hold values from 1 to 48, as said below
- send_x: int32 [256, 2, 64], P(('gx', 'gy')), may hold values from 0 to 127
- send_y: int32 [256, 2, 128], P(('gx', 'gy')), may hold values from 0 to 255
- embed: bfloat16 [10, 128], replicated, may hold values from -6 to 6
- radial_w: float32 [2, 8, 128], replicated, may hold values from -2 to 2
- update_w: bfloat16 [2, 384, 128], replicated, may hold values from -0.3125 to 0.3125
- out_w: float32 [128], replicated, may hold values from -0.5 to 0.5
Outputs:
- atom_energy: float32 [32768], P(('gx', 'gy'))
- forces: float32 [3, 32768], P(None, ('gx', 'gy'))
Inputs may be any that keep to these rules, and one draw needn't show every extreme that they name: `positions`: every coordinate is a multiple of 1/16 in [0, 8). `counts`: some atom has all 48 slots live.
All inputs are finite; a program needn't handle non-finite values.
Results may differ from a plain program's by a relative error of at most 0.012.
The roundings to bfloat16 on the way count: a program that leaves them out, or rounds other values in their place, can miss the bound.
Values may be sent and summed in bfloat16 or wider, within the bound.
A program may use at most 64 MiB of HBM per device.

v0:
```python
import math

import jax
import jax.numpy as jnp
from jax import lax
from jax.sharding import PartitionSpec as P

NB = 8


BOX = 8.0
SCALE = 0.25
HIGH = lax.Precision.HIGHEST


def from_behind(value, axis, steps):
    count = lax.axis_size(axis)
    pairs = [(source, (source + steps) % count) for source in range(count)]
    return lax.ppermute(value, axis, pairs)


def geometry(rel):
    dist = jnp.sqrt(jnp.sum(rel * rel, axis=0) + 1.0)
    unit_x = rel[0] / dist
    unit_y = rel[1] / dist
    unit_z = rel[2] / dist
    root3 = math.sqrt(3.0)
    root5 = math.sqrt(5.0)
    root15 = math.sqrt(15.0)
    harm = jnp.stack(
        [
            jnp.ones_like(dist),
            root3 * unit_x,
            root3 * unit_y,
            root3 * unit_z,
            root15 * unit_x * unit_y,
            root15 * unit_y * unit_z,
            0.5 * root5 * (3.0 * unit_z * unit_z - 1.0),
            root15 * unit_x * unit_z,
            0.5 * root15 * (unit_x * unit_x - unit_y * unit_y),
        ],
        0,
    )
    centers = 1.0 + 2.0 * jnp.arange(NB).astype(dist.dtype)[:, None]
    basis = jnp.exp(-0.125 * (dist[None, :] - centers) ** 2)
    return (harm, basis)


def invariants(amps):
    return jnp.concatenate(
        [
            amps[:, 0:1],
            jnp.sum(amps[:, 1:4] ** 2, axis=1, keepdims=True),
            jnp.sum(amps[:, 4:9] ** 2, axis=1, keepdims=True),
        ],
        1,
    )


def invariant_grads(amps, grad_inv):
    return jnp.concatenate(
        [
            grad_inv[:, 0:1],
            2.0 * amps[:, 1:4] * grad_inv[:, 1:2],
            2.0 * amps[:, 4:9] * grad_inv[:, 2:3],
        ],
        1,
    )


def silu_slope(z):
    sig = jax.nn.sigmoid(z)
    return sig * (1.0 + z * (1.0 - sig))


def update(amps, h_own, weights):
    flat = invariants(amps).reshape(amps.shape[0], -1).astype(jnp.bfloat16)
    z = jnp.dot(flat, weights, preferred_element_type=jnp.float32)
    return (z, (h_own.astype(jnp.float32) + jax.nn.silu(z)).astype(jnp.bfloat16))


def back_update(z, grad_h, weights):
    grad_z = grad_h * silu_slope(z)
    grad_inv = jnp.dot(grad_z, weights.astype(jnp.float32).T, precision=HIGH)
    return grad_inv.reshape(z.shape[0], 3, -1)


def embed_rows(spc, embed):
    count = embed.shape[0]
    onehot = (spc[:, None] == jnp.arange(count).astype(jnp.bfloat16)[None, :]).astype(jnp.bfloat16)
    return jnp.dot(onehot, embed, preferred_element_type=jnp.float32).astype(jnp.bfloat16)


def selector(index, total, dtype):
    return (index[:, None] == jnp.arange(total, dtype=jnp.int32)[None, :]).astype(dtype)


def pick_rows(table, index):
    chosen = selector(index, table.shape[0], jnp.bfloat16)
    return jnp.dot(chosen, table, preferred_element_type=jnp.float32)


def pick_columns(table, index):
    chosen = selector(index, table.shape[1], jnp.bfloat16)
    return jnp.einsum("dn,en->de", table, chosen, preferred_element_type=jnp.float32)


def block_layout(rel, nbr, live, rows_block, slots):
    span = rows_block * slots
    blocks = nbr.shape[0] // span
    return (
        rel.reshape(3, blocks, span).transpose(1, 0, 2),
        nbr.reshape(blocks, span),
        live.reshape(blocks, span),
    )


def block_sums(rel, nbr, live, h_ext, weights, rows_block, slots):

    def one_block(inputs):
        rel_b, nbr_b, live_b = inputs
        harm, basis = geometry(rel_b)
        radial = jnp.einsum("be,bc->ec", basis, weights, precision=HIGH)
        gathered = pick_rows(h_ext, nbr_b)
        message = radial * gathered * live_b[:, None]
        width = message.shape[1]
        return SCALE * jnp.einsum(
            "lnk,nkc->nlc",
            harm.reshape(9, rows_block, slots),
            message.reshape(rows_block, slots, width),
            precision=HIGH,
        )

    amps = lax.map(one_block, block_layout(rel, nbr, live, rows_block, slots))
    return amps.reshape(-1, 9, amps.shape[-1])


def block_grads(rel, nbr, live, grad_amps, h_ext, weights, rows_block, slots, extended, features):
    rel_s, nbr_s, live_s = block_layout(rel, nbr, live, rows_block, slots)
    blocks = nbr_s.shape[0]
    width = h_ext.shape[1]
    grad_s = grad_amps.reshape(blocks, rows_block, 9, width)
    starts = jnp.arange(blocks, dtype=jnp.int32) * rows_block

    def one_block(carry, inputs):
        rel_b, nbr_b, live_b, grad_b, start = inputs
        (harm, basis), back = jax.vjp(geometry, rel_b)
        radial = jnp.einsum("be,bc->ec", basis, weights, precision=HIGH)
        chosen = selector(nbr_b, extended, jnp.float32)
        gathered = jnp.dot(chosen.astype(jnp.bfloat16), h_ext, preferred_element_type=jnp.float32)
        message = radial * gathered * live_b[:, None]
        harm3 = harm.reshape(9, rows_block, slots)
        grad_msg = SCALE * jnp.einsum("lnk,nlc->nkc", harm3, grad_b, precision=HIGH).reshape(
            -1, width
        )
        grad_harm = SCALE * jnp.einsum(
            "nlc,nkc->lnk", grad_b, message.reshape(rows_block, slots, width), precision=HIGH
        ).reshape(9, -1)
        grad_radial = grad_msg * gathered * live_b[:, None]
        grad_basis = jnp.einsum("ec,bc->be", grad_radial, weights, precision=HIGH)
        grad_rel = back((grad_harm, grad_basis))[0]
        grad_pos = carry[0] + jnp.einsum("de,en->dn", grad_rel, chosen, precision=HIGH)
        own_sum = jnp.sum(grad_rel.reshape(3, rows_block, slots), axis=2)
        current = lax.dynamic_slice_in_dim(grad_pos, start, rows_block, 1)
        grad_pos = lax.dynamic_update_slice_in_dim(grad_pos, current - own_sum, start, 1)
        if features:
            added = jnp.einsum(
                "en,ec->nc", chosen, grad_msg * radial * live_b[:, None], precision=HIGH
            )
            return ((grad_pos, carry[1] + added), None)
        return ((grad_pos,), None)

    init = (jnp.zeros((3, extended), jnp.float32),)
    if features:
        init = init + (jnp.zeros((extended, width), jnp.float32),)
    carry, unused = lax.scan(one_block, init, (rel_s, nbr_s, live_s, grad_s, starts))
    return carry


def take_along(arr, axis, index):
    if axis == 0:
        return pick_rows(arr, index).astype(arr.dtype)
    return pick_columns(arr, index).astype(arr.dtype)


def spread(arr, axis, send_x, send_y, shifted):
    pieces = (take_along(arr, axis, send_x[0, 0]), take_along(arr, axis, send_x[0, 1]))
    got = []
    for by, piece in zip((1, -1), pieces):
        got.append(from_behind(piece, "gx", by))
    if shifted:
        got = [
            got[0].at[0].add(jnp.asarray(-BOX, got[0].dtype)),
            got[1].at[0].add(jnp.asarray(BOX, got[1].dtype)),
        ]
    section = jnp.concatenate([arr] + got, axis)
    pieces = (take_along(section, axis, send_y[0, 0]), take_along(section, axis, send_y[0, 1]))
    got = []
    for by, piece in zip((1, -1), pieces):
        got.append(from_behind(piece, "gy", by))
    if shifted:
        got = [
            got[0].at[1].add(jnp.asarray(-BOX, got[0].dtype)),
            got[1].at[1].add(jnp.asarray(BOX, got[1].dtype)),
        ]
    return jnp.concatenate([section] + got, axis)


def cut(arr, axis, start, size):
    return lax.slice_in_dim(arr, start, start + size, axis=axis)


def add_at(base, axis, index, values):
    chosen = selector(index, base.shape[axis], jnp.float32)
    if axis == 0:
        return base + jnp.einsum("en,ec->nc", chosen, values, precision=HIGH)
    return base + jnp.einsum("de,en->dn", values, chosen, precision=HIGH)


def give_back(items, send_x, send_y, owned):
    side_x = send_x.shape[2]
    side_y = send_y.shape[2]
    first = owned + 2 * side_x
    bases = [cut(arr, axis, 0, first) for arr, axis in items]
    for by, which, start in ((-1, 0, first), (1, 1, first + side_y)):
        pieces = tuple((cut(arr, axis, start, side_y) for arr, axis in items))
        got = from_behind(pieces, "gy", by)
        bases = [
            add_at(base, item[1], send_y[0, which], piece)
            for base, item, piece in zip(bases, items, got)
        ]
    owns = [cut(base, item[1], 0, owned) for base, item in zip(bases, items)]
    for by, which, start in ((-1, 0, owned), (1, 1, owned + side_x)):
        pieces = tuple((cut(base, item[1], start, side_x) for base, item in zip(bases, items)))
        got = from_behind(pieces, "gx", by)
        owns = [
            add_at(own, item[1], send_x[0, which], piece)
            for own, item, piece in zip(owns, items, got)
        ]
    return owns


def body(positions, species, neighbours, counts, send_x, send_y, embed, radial_w, update_w, out_w):
    owned = positions.shape[1]
    slots = neighbours.shape[1]
    width = embed.shape[1]
    rows_block = min(128, owned)
    geo = jnp.concatenate([positions, species.astype(jnp.bfloat16)[None, :]], 0)
    geo_ext = spread(geo, 1, send_x, send_y, True)
    extended = geo_ext.shape[1]
    pos_ext = geo_ext[:3].astype(jnp.float32)
    nbr = neighbours.reshape(-1)
    rel = jnp.take(pos_ext, nbr, axis=1) - jnp.repeat(pos_ext[:, :owned], slots, axis=1)
    live = (jnp.arange(slots)[None, :] < counts[:, None]).astype(jnp.float32).reshape(-1)
    h0_ext = embed_rows(geo_ext[3], embed)
    amps_one = block_sums(rel, nbr, live, h0_ext, radial_w[0], rows_block, slots)
    z_one, h_one = update(amps_one, h0_ext[:owned], update_w[0])
    h1_ext = spread(h_one, 0, send_x, send_y, False)
    amps_two = block_sums(rel, nbr, live, h1_ext, radial_w[1], rows_block, slots)
    z_two, h_two = update(amps_two, h1_ext[:owned], update_w[1])
    energy = jnp.dot(h_two.astype(jnp.float32), out_w, precision=HIGH)
    grad_h = jnp.broadcast_to(out_w, (owned, width))
    grad_amps = invariant_grads(amps_two, back_update(z_two, grad_h, update_w[1]))
    grad_two, grad_feat = block_grads(
        rel, nbr, live, grad_amps, h1_ext, radial_w[1], rows_block, slots, extended, True
    )
    grad_feat = grad_feat.at[:owned].add(grad_h)
    grad_h1, pos_two = give_back(((grad_feat, 0), (grad_two, 1)), send_x, send_y, owned)
    grad_first = invariant_grads(amps_one, back_update(z_one, grad_h1, update_w[0]))
    grad_one = block_grads(
        rel, nbr, live, grad_first, h0_ext, radial_w[0], rows_block, slots, extended, False
    )[0]
    pos_one = give_back(((grad_one, 1),), send_x, send_y, owned)[0]
    total = pos_one + pos_two
    return (energy, -total)


def solution(mesh):
    return jax.shard_map(
        body,
        mesh=mesh,
        in_specs=(
            P(None, ("gx", "gy")),
            P(("gx", "gy")),
            P(("gx", "gy"), None),
            P(("gx", "gy")),
            P(("gx", "gy"), None, None),
            P(("gx", "gy"), None, None),
            P(),
            P(),
            P(),
            P(),
        ),
        out_specs=(P(("gx", "gy")), P(None, ("gx", "gy"))),
        check_vma=False,
    )
```

profile of v0, /device:TPU:24, one launch (start us, length us, event | category | flops | bytes accessed | tf_op | source)
XLA Modules:
  0.0 245.4 jit_solution(12662483808120942517)
XLA Ops:
  3.2 6.3 %collective-permute-start.1 = (bf16[4,64]{1,0:T(4,128)(2,1)S(1)}, bf16[4,64]{1,0:T(4,128)(2,1)S(1)}, u32[]{:S(2)}, u32[]{:S(2)}) collective-permute-start(bf16[4,64]{1,0:T(4,128)(2,1)S(1)} %convolution_convert_fusion.5), channel_id=1, source_target_pairs={{0,248},{8,0},{16,8},{24,16},{32,24},{40,32},{48,40},{56,48},{64,5... | collective-permute-start | bytes 1544 | tf_op jit(solution)/shard_map/ppermute | solution.py:19
  17.5 6.3 %collective-permute-start.2 = (bf16[4,128]{1,0:T(4,128)(2,1)S(1)}, bf16[4,128]{1,0:T(4,128)(2,1)S(1)}, u32[]{:S(2)}, u32[]{:S(2)}) collective-permute-start(bf16[4,128]{1,0:T(4,128)(2,1)S(1)} %convolution_convert_fusion.8), channel_id=1, source_target_pairs={{0,1},{1,2},{2,3},{3,4},{4,5},{5,6},{6,7},{7,0},{8,9},{9,10},{10,1... | collective-permute-start | bytes 3080 | tf_op jit(solution)/shard_map/ppermute | solution.py:19
  25.1 8.5 %collective-permute-done.3 = bf16[4,128]{1,0:T(4,128)(2,1)S(1)} collective-permute-done((bf16[4,128]{1,0:T(4,128)(2,1)S(1)}, bf16[4,128]{1,0:T(4,128)(2,1)S(1)}, u32[]{:S(2)}, u32[]{:S(2)}) %collective-permute-start.3) | collective-permute-done | bytes 1056 | tf_op jit(solution)/shard_map/ppermute | solution.py:19
  35.6 16.1 %gather_fusion = f32[6144,3]{1,0:T(8,128)S(1)} fusion(f32[3,512]{0,1:T(8,128)S(1)} %copy.255, s32[6144]{0:T(1024)S(1)} %broadcast_clamp_fusion), kind=kCustom, calls=%fused_computation | custom fusion | bytes 172032 | tf_op jit(solution)/shard_map/jit(_take)/gather | solution.py:253
  54.8 5.1 %fusion.39 = f32[6144,128]{1,0:T(8,128)S(1)} fusion(f32[8]{0:T(128)S(1)} %multiply_add_fusion.8, f32[6144]{0:T(1024)S(1)} %get-tuple-element.234, f32[2,8,128]{2,1,0:T(8,128)S(1)} %copy-done.23), kind=kOutput, calls=%fused_computation.79 | convolution fusion | flops 75644928 | bytes 3174912 | tf_op jit(solution)/shard_map/while/body/eval_jaxpr/be,bc->ec/dot_general | solution.py:123
  60.3 6.5 %fusion.10 = f32[6144,128]{1,0:T(8,128)} fusion(f32[6144,128]{1,0:T(8,128)S(1)} %fusion.39, bf16[512,128]{1,0:T(8,128)(2,1)S(1)} %convolution_convert_fusion, s32[6144]{0:T(1024)S(1)} %reshape.468, f32[6144]{0:T(1024)S(1)} %copy-done.5), kind=kOutput, calls=%fused_computation.13 | convolution fusion | flops 810024960 | bytes 6471680 | tf_op jit(solution)/shard_map/while/body/eval_jaxpr/dot_general | solution.py:100
  68.1 4.8 %convolution_multiply_fusion.5 = f32[128,9,128]{2,1,0:T(8,128)S(1)} fusion(f32[9,128,48]{2,0,1:T(8,128)S(1)} %stack.101, f32[128,48,128]{2,1,0:T(8,128)} %bitcast.188), kind=kOutput, calls=%fused_computation.44 | convolution fusion | flops 85082112 | bytes 3956736 | tf_op jit(solution)/shard_map/while/body/eval_jaxpr/lnk,nkc->nlc/dot_general | solution.py:127
  75.1 5.6 %collective-permute-start.5 = (bf16[64,128]{1,0:T(8,128)(2,1)S(1)}, bf16[64,128]{1,0:T(8,128)(2,1)S(1)}, u32[]{:S(2)}, u32[]{:S(2)}) collective-permute-start(bf16[64,128]{1,0:T(8,128)(2,1)S(1)} %convolution_convert_fusion.3), channel_id=1, source_target_pairs={{0,248},{8,0},{16,8},{24,16},{32,24},{40,32},{48,40},{56,48},{64,5... | collective-permute-start | bytes 49160 | tf_op jit(solution)/shard_map/ppermute | solution.py:19
  80.8 5.1 %fusion.37 = f32[6144,128]{1,0:T(8,128)S(1)} fusion(f32[8]{0:T(128)S(1)} %multiply_add_fusion.8, f32[6144]{0:T(1024)S(1)} %get-tuple-element.234, f32[2,8,128]{2,1,0:T(8,128)S(1)} %copy-done.23), kind=kOutput, calls=%fused_computation.78 | convolution fusion | flops 75644928 | bytes 3174912 | tf_op jit(solution)/shard_map/while/body/eval_jaxpr/be,bc->ec/dot_general | solution.py:123
  86.5 2.5 %collective-permute-start.7 = (bf16[128,128]{1,0:T(8,128)(2,1)S(1)}, bf16[128,128]{1,0:T(8,128)(2,1)S(1)}, u32[]{:S(2)}, u32[]{:S(2)}) collective-permute-start(bf16[128,128]{1,0:T(8,128)(2,1)S(1)} %convolution_convert_fusion.1), channel_id=1, source_target_pairs={{0,7},{1,0},{2,1},{3,2},{4,3},{5,4},{6,5},{7,6},{8,15},{9,8},{10,9... | collective-permute-start | bytes 98312 | tf_op jit(solution)/shard_map/ppermute | solution.py:19
  90.1 6.7 %collective-permute-done.7 = bf16[128,128]{1,0:T(8,128)(2,1)S(1)} collective-permute-done((bf16[128,128]{1,0:T(8,128)(2,1)S(1)}, bf16[128,128]{1,0:T(8,128)(2,1)S(1)}, u32[]{:S(2)}, u32[]{:S(2)}) %collective-permute-start.7) | collective-permute-done | bytes 32800 | tf_op jit(solution)/shard_map/ppermute | solution.py:19
  96.9 6.0 %fusion.9 = f32[6144,128]{1,0:T(8,128)S(1)} fusion(f32[6144,128]{1,0:T(8,128)S(1)} %fusion.37, bf16[512,128]{1,0:T(8,128)(2,1)S(1)} %constant_dynamic-update-slice_fusion, s32[6144]{0:T(1024)S(1)} %reshape.468, f32[6144]{0:T(1024)S(1)} %copy-done.5), kind=kOutput, calls=%fused_computation.12 | convolution fusion | flops 810024960 | bytes 6471680 | tf_op jit(solution)/shard_map/while/body/eval_jaxpr/dot_general | solution.py:100
  103.0 3.0 %convolution_multiply_fusion.4 = f32[128,9,128]{2,1,0:T(8,128)S(1)} fusion(f32[9,128,48]{2,0,1:T(8,128)S(1)} %stack.101, f32[128,48,128]{2,1,0:T(8,128)S(1)} %bitcast.189), kind=kOutput, calls=%fused_computation.43 | convolution fusion | flops 85082112 | bytes 3956736 | tf_op jit(solution)/shard_map/while/body/eval_jaxpr/lnk,nkc->nlc/dot_general | solution.py:127
  110.7 5.1 %convolution_multiply_fusion.1 = f32[128,48,128]{2,1,0:T(8,128)S(1)} fusion(f32[9,128,48]{2,0,1:T(8,128)S(1)} %stack.101, f32[128,5,128]{2,1,0:T(8,128)S(1)} %slice_multiply_fusion, f32[128,3,128]{2,1,0:T(4,128)S(1)} %slice_multiply_fusion.2, f32[128,1,128]{2,1,0:T(1,128)S(1)} %bitcast.193), kind=kOutput, calls=%fused_computation.38 | convolution fusion | flops 86016000 | bytes 3956736 | tf_op jit(solution)/shard_map/while/body/eval_jaxpr/lnk,nlc->nkc/dot_general | solution.py:153
  115.9 6.9 %fusion.25 = (f32[6144,128]{1,0:T(8,128)S(1)}, f32[6144,128]{1,0:T(8,128)S(1)}, f32[6144,128]{1,0:T(8,128)S(1)}) fusion(f32[6144,128]{1,0:T(8,128)S(1)} %copy-done.2, f32[128,48,128]{2,1,0:T(8,128)S(1)} %convolution_multiply_fusion.1, f32[6144]{0:T(1024)S(1)} %copy-done.5, bf16[512,128]{1,0:T(8,128)(2,1)S(1)} %copy-done.21, s32[6144]{0:T(1024)S(1)} %reshape.468), kind=kOutput, calls=%fused_computation.33 | convolution fusion | flops 819462144 | bytes 15908864 | tf_op jit(solution)/shard_map/while/body/eval_jaxpr/dot_general | solution.py:150
  122.7 10.8 %fusion.2 = f32[512,128]{1,0:T(8,128)S(1)} fusion(f32[6144,128]{1,0:T(8,128)S(1)} %get-tuple-element.186, s32[6144]{0:T(1024)S(1)} %reshape.468), kind=kOutput, calls=%fused_computation.5 | convolution fusion | flops 4834983936 | bytes 3432448 | tf_op jit(solution)/shard_map/while/body/eval_jaxpr/en,ec->nc/dot_general | solution.py:167
  133.6 3.8 %fusion.30 = f32[6144]{0:T(1024)} fusion(f32[6144,128]{1,0:T(8,128)S(1)} %get-tuple-element.187, f32[8]{0:T(128)S(1)} %multiply_add_fusion.8, f32[6144]{0:T(1024)S(1)} %get-tuple-element.234, f32[2,8,128]{2,1,0:T(8,128)S(1)} %copy-done.23), kind=kOutput, calls=%fused_computation.48 | convolution fusion | flops 75884544 | bytes 3199488 | tf_op jit(solution)/shard_map/while/body/eval_jaxpr/ec,bc->be/dot_general | solution.py:160
  138.0 8.0 %collective-permute-start.9 = (f32[128,128]{1,0:T(8,128)}, f32[128,128]{1,0:T(8,128)}, u32[]{:S(2)}, u32[]{:S(2)}) collective-permute-start(f32[128,128]{1,0:T(8,128)} %get-tuple-element.206), channel_id=1, source_target_pairs={{0,1},{1,2},{2,3},{3,4},{4,5},{5,6},{6,7},{7,0},{8,9},{9,10},{10,1... | collective-permute-start | bytes 196616 | tf_op jit(solution)/shard_map/ppermute | solution.py:19
  146.1 5.1 %fusion.27 = f32[9,128,48]{2,0,1:T(8,128)S(1)} fusion(f32[128,48,128]{2,1,0:T(8,128)S(1)} %bitcast.184, f32[128,5,128]{2,1,0:T(8,128)S(1)} %slice_multiply_fusion, f32[128,3,128]{2,1,0:T(4,128)S(1)} %slice_multiply_fusion.2, f32[128,1,128]{2,1,0:T(1,128)S(1)} %bitcast.194), kind=kOutput, calls=%fused_computation.40 | convolution fusion | flops 85284864 | bytes 3956736 | tf_op jit(solution)/shard_map/while/body/eval_jaxpr/nlc,nkc->lnk/dot_general | solution.py:156
  151.2 2.3 fusion.183
  168.3 6.7 %collective-permute-done.11 = f32[64,128]{1,0:T(8,128)S(1)} collective-permute-done((f32[64,128]{1,0:T(8,128)S(1)}, f32[64,128]{1,0:T(8,128)S(1)}, u32[]{:S(2)}, u32[]{:S(2)}) %collective-permute-start.11) | collective-permute-done | bytes 32800 | tf_op jit(solution)/shard_map/ppermute | solution.py:19
  176.7 5.1 %convolution_multiply_fusion = f32[128,48,128]{2,1,0:T(8,128)S(1)} fusion(f32[9,128,48]{2,0,1:T(8,128)S(1)} %stack.101, f32[128,5,128]{2,1,0:T(8,128)S(1)} %slice_multiply_fusion.1, f32[128,3,128]{2,1,0:T(4,128)S(1)} %slice_multiply_fusion.3, f32[128,1,128]{2,1,0:T(1,128)S(1)} %bitcast.195), kind=kOutput, calls=%fused_computation.37 | convolution fusion | flops 86016000 | bytes 3956736 | tf_op jit(solution)/shard_map/while/body/eval_jaxpr/lnk,nlc->nkc/dot_general | solution.py:153
  181.8 6.0 %fusion.24 = (f32[6144,128]{1,0:T(8,128)S(1)}, f32[6144,128]{1,0:T(8,128)S(1)}) fusion(f32[128,48,128]{2,1,0:T(8,128)S(1)} %convolution_multiply_fusion, f32[6144]{0:T(1024)S(1)} %copy-done.5, f32[6144,128]{1,0:T(8,128)S(1)} %copy-done.4, bf16[512,128]{1,0:T(8,128)(2,1)S(1)} %copy-done.19, s32[6144]{0:T(1024)S(1)} %reshape.468), kind=kOutput, calls=%fused_computation.30 | convolution fusion | flops 817889280 | bytes 12763136 | tf_op jit(solution)/shard_map/while/body/eval_jaxpr/dot_general | solution.py:150
  187.8 2.8 %fusion.31 = f32[6144]{0:T(1024)S(1)} fusion(f32[6144,128]{1,0:T(8,128)S(1)} %get-tuple-element.184, f32[8]{0:T(128)S(1)} %multiply_add_fusion.8, f32[6144]{0:T(1024)S(1)} %get-tuple-element.234, f32[2,8,128]{2,1,0:T(8,128)S(1)} %copy-done.23), kind=kOutput, calls=%fused_computation.49 | convolution fusion | flops 75884544 | bytes 3199488 | tf_op jit(solution)/shard_map/while/body/eval_jaxpr/ec,bc->be/dot_general | solution.py:160
  190.7 5.1 %fusion.28 = f32[9,128,48]{2,0,1:T(8,128)S(1)} fusion(f32[128,48,128]{2,1,0:T(8,128)S(1)} %bitcast.185, f32[128,5,128]{2,1,0:T(8,128)S(1)} %slice_multiply_fusion.1, f32[128,3,128]{2,1,0:T(4,128)S(1)} %slice_multiply_fusion.3, f32[128,1,128]{2,1,0:T(1,128)S(1)} %bitcast.196), kind=kOutput, calls=%fused_computation.42 | convolution fusion | flops 85284864 | bytes 3956736 | tf_op jit(solution)/shard_map/while/body/eval_jaxpr/nlc,nkc->lnk/dot_general | solution.py:156
  199.8 4.2 %fusion = f32[3,512]{1,0:T(4,128)S(1)} fusion(f32[3,6144]{1,0:T(4,128)S(1)} %get-tuple-element.226, s32[6144]{0:T(1024)S(1)} %reshape.468), kind=kOutput, calls=%fused_computation.3 | convolution fusion | flops 116391936 | bytes 104448 | tf_op jit(solution)/shard_map/while/body/eval_jaxpr/de,en->dn/dot_general | solution.py:162
  206.1 4.0 %fusion.1 = f32[3,512]{1,0:T(4,128)S(1)} fusion(f32[3,6144]{1,0:T(4,128)S(1)} %get-tuple-element.225, s32[6144]{0:T(1024)S(1)} %reshape.468), kind=kOutput, calls=%fused_computation.4 | convolution fusion | flops 116391936 | bytes 104448 | tf_op jit(solution)/shard_map/while/body/eval_jaxpr/de,en->dn/dot_general | solution.py:162
  211.2 2.3 reduce_sum.119
  213.7 8.0 %collective-permute-start.17 = (f32[3,128]{1,0:T(4,128)S(1)}, f32[3,128]{1,0:T(4,128)S(1)}, u32[]{:S(2)}, u32[]{:S(2)}) collective-permute-start(f32[3,128]{1,0:T(4,128)S(1)} %get-tuple-element.239), channel_id=1, source_target_pairs={{0,1},{1,2},{2,3},{3,4},{4,5},{5,6},{6,7},{7,0},{8,9},{9,10},{10,1... | collective-permute-start | bytes 4616 | tf_op jit(solution)/shard_map/ppermute | solution.py:19
  222.4 8.0 %collective-permute-start.13 = (f32[3,128]{1,0:T(4,128)S(1)}, f32[3,128]{1,0:T(4,128)S(1)}, u32[]{:S(2)}, u32[]{:S(2)}) collective-permute-start(f32[3,128]{1,0:T(4,128)S(1)} %get-tuple-element.237), channel_id=1, source_target_pairs={{0,1},{1,2},{2,3},{3,4},{4,5},{5,6},{6,7},{7,0},{8,9},{9,10},{10,1... | collective-permute-start | bytes 4616 | tf_op jit(solution)/shard_map/ppermute | solution.py:19
  232.2 5.0 %collective-permute-start.14 = (f32[3,64]{1,0:T(4,128)S(1)}, f32[3,64]{1,0:T(4,128)S(1)}, u32[]{:S(2)}, u32[]{:S(2)}) collective-permute-start(f32[3,64]{1,0:T(4,128)S(1)} %get-tuple-element.240), channel_id=1, source_target_pairs={{0,248},{8,0},{16,8},{24,16},{32,24},{40,32},{48,40},{56,48},{64,5... | collective-permute-start | bytes 2312 | tf_op jit(solution)/shard_map/ppermute | solution.py:19
  238.7 5.4 %collective-permute-done.15 = f32[3,64]{1,0:T(4,128)S(1)} collective-permute-done((f32[3,64]{1,0:T(4,128)S(1)}, f32[3,64]{1,0:T(4,128)S(1)}, u32[]{:S(2)}, u32[]{:S(2)}) %collective-permute-start.15) | collective-permute-done | bytes 800 | tf_op jit(solution)/shard_map/ppermute | solution.py:19
  (256 shorter events, 56.2 us)
Async XLA Ops:
  0.6 59.3 %copy-start = (bf16[10,128]{1,0:T(8,128)(2,1)S(1)}, bf16[10,128]{1,0:T(8,128)(2,1)}, u32[]{:S(2)}) copy-start(bf16[10,128]{1,0:T(8,128)(2,1)} %param.26) | copy-start | bytes 7684
  3.0 13.5 %collective-permute-start = (bf16[4,64]{1,0:T(4,128)(2,1)S(1)}, bf16[4,64]{1,0:T(4,128)(2,1)S(1)}, u32[]{:S(2)}, u32[]{:S(2)}) collective-permute-start(bf16[4,64]{1,0:T(4,128)(2,1)S(1)} %convolution_convert_fusion.6), channel_id=1, source_target_pairs={{0,8},{8,16},{16,24},{24,32},{32,40},{40,48},{48,56},{56,64},{64,7... | collective-permute-start | bytes 1544 | tf_op jit(solution)/shard_map/ppermute | solution.py:19
  3.2 13.3 %collective-permute-start.1 = (bf16[4,64]{1,0:T(4,128)(2,1)S(1)}, bf16[4,64]{1,0:T(4,128)(2,1)S(1)}, u32[]{:S(2)}, u32[]{:S(2)}) collective-permute-start(bf16[4,64]{1,0:T(4,128)(2,1)S(1)} %convolution_convert_fusion.5), channel_id=1, source_target_pairs={{0,248},{8,0},{16,8},{24,16},{32,24},{40,32},{48,40},{56,48},{64,5... | collective-permute-start | bytes 1544 | tf_op jit(solution)/shard_map/ppermute | solution.py:19
  12.0 39.7 %copy-start.29 = (s32[128]{0:T(128)}, s32[128]{0:T(128)S(1)}, u32[]{:S(2)}) copy-start(s32[128]{0:T(128)S(1)} %get-tuple-element.244) | copy-start | bytes 1540
  12.0 39.7 %copy-start.32 = (s32[128]{0:T(128)}, s32[128]{0:T(128)S(1)}, u32[]{:S(2)}) copy-start(s32[128]{0:T(128)S(1)} %get-tuple-element.245) | copy-start | bytes 1540
  17.5 7.6 %collective-permute-start.2 = (bf16[4,128]{1,0:T(4,128)(2,1)S(1)}, bf16[4,128]{1,0:T(4,128)(2,1)S(1)}, u32[]{:S(2)}, u32[]{:S(2)}) collective-permute-start(bf16[4,128]{1,0:T(4,128)(2,1)S(1)} %convolution_convert_fusion.8), channel_id=1, source_target_pairs={{0,1},{1,2},{2,3},{3,4},{4,5},{5,6},{6,7},{7,0},{8,9},{9,10},{10,1... | collective-permute-start | bytes 3080 | tf_op jit(solution)/shard_map/ppermute | solution.py:19
  24.0 9.6 %collective-permute-start.3 = (bf16[4,128]{1,0:T(4,128)(2,1)S(1)}, bf16[4,128]{1,0:T(4,128)(2,1)S(1)}, u32[]{:S(2)}, u32[]{:S(2)}) collective-permute-start(bf16[4,128]{1,0:T(4,128)(2,1)S(1)} %convolution_convert_fusion.7), channel_id=1, source_target_pairs={{0,7},{1,0},{2,1},{3,2},{4,3},{5,4},{6,5},{7,6},{8,15},{9,8},{10,9... | collective-permute-start | bytes 3080 | tf_op jit(solution)/shard_map/ppermute | solution.py:19
  34.7 20.1 %copy-start.23 = (f32[2,8,128]{2,1,0:T(8,128)S(1)}, f32[2,8,128]{2,1,0:T(8,128)}, u32[]{:S(2)}) copy-start(f32[2,8,128]{2,1,0:T(8,128)} %param.27) | copy-start | bytes 24580
  53.1 109.4 %copy-start.9 = (f32[6144]{0:T(1024)}, f32[6144]{0:T(1024)S(1)}, u32[]{:S(2)}) copy-start(f32[6144]{0:T(1024)S(1)} %get-tuple-element.216) | copy-start | bytes 73732
  54.1 107.3 %copy-start.11 = (f32[1,6144]{1,0:T(1,128)}, f32[1,6144]{1,0:T(1,128)S(1)}, u32[]{:S(2)}) copy-start(f32[1,6144]{1,0:T(1,128)S(1)} %get-tuple-element.181) | copy-start | bytes 73732
  60.3 13.6 %copy-start.18 = (bf16[512,128]{1,0:T(8,128)(2,1)}, bf16[512,128]{1,0:T(8,128)(2,1)S(1)}, u32[]{:S(2)}) copy-start(bf16[512,128]{1,0:T(8,128)(2,1)S(1)} %convolution_convert_fusion) | copy-start | bytes 393220
  74.7 28.2 %copy-start.38 = (bf16[128,128]{1,0:T(8,128)(2,1)}, bf16[128,128]{1,0:T(8,128)(2,1)S(1)}, u32[]{:S(2)}) copy-start(bf16[128,128]{1,0:T(8,128)(2,1)S(1)} %get-tuple-element.180) | copy-start | bytes 98308
  75.1 10.8 %collective-permute-start.4 = (bf16[64,128]{1,0:T(8,128)(2,1)S(1)}, bf16[64,128]{1,0:T(8,128)(2,1)S(1)}, u32[]{:S(2)}, u32[]{:S(2)}) collective-permute-start(bf16[64,128]{1,0:T(8,128)(2,1)S(1)} %convolution_convert_fusion.4), channel_id=1, source_target_pairs={{0,8},{8,16},{16,24},{24,32},{32,40},{40,48},{48,56},{56,64},{64,7... | collective-permute-start | bytes 49160 | tf_op jit(solution)/shard_map/ppermute | solution.py:19
  75.1 10.8 %collective-permute-start.5 = (bf16[64,128]{1,0:T(8,128)(2,1)S(1)}, bf16[64,128]{1,0:T(8,128)(2,1)S(1)}, u32[]{:S(2)}, u32[]{:S(2)}) collective-permute-start(bf16[64,128]{1,0:T(8,128)(2,1)S(1)} %convolution_convert_fusion.3), channel_id=1, source_target_pairs={{0,248},{8,0},{16,8},{24,16},{32,24},{40,32},{48,40},{56,48},{64,5... | collective-permute-start | bytes 49160 | tf_op jit(solution)/shard_map/ppermute | solution.py:19
  85.9 17.0 %copy-start.1 = (f32[6144,128]{1,0:T(8,128)}, f32[6144,128]{1,0:T(8,128)S(1)}, u32[]{:S(2)}) copy-start(f32[6144,128]{1,0:T(8,128)S(1)} %fusion.37) | copy-start | bytes 9437188
  86.1 4.0 %collective-permute-start.6 = (bf16[128,128]{1,0:T(8,128)(2,1)S(1)}, bf16[128,128]{1,0:T(8,128)(2,1)S(1)}, u32[]{:S(2)}, u32[]{:S(2)}) collective-permute-start(bf16[128,128]{1,0:T(8,128)(2,1)S(1)} %convolution_convert_fusion.2), channel_id=1, source_target_pairs={{0,1},{1,2},{2,3},{3,4},{4,5},{5,6},{6,7},{7,0},{8,9},{9,10},{10,1... | collective-permute-start | bytes 98312 | tf_op jit(solution)/shard_map/ppermute | solution.py:19
  86.5 10.4 %collective-permute-start.7 = (bf16[128,128]{1,0:T(8,128)(2,1)S(1)}, bf16[128,128]{1,0:T(8,128)(2,1)S(1)}, u32[]{:S(2)}, u32[]{:S(2)}) collective-permute-start(bf16[128,128]{1,0:T(8,128)(2,1)S(1)} %convolution_convert_fusion.1), channel_id=1, source_target_pairs={{0,7},{1,0},{2,1},{3,2},{4,3},{5,4},{6,5},{7,6},{8,15},{9,8},{10,9... | collective-permute-start | bytes 98312 | tf_op jit(solution)/shard_map/ppermute | solution.py:19
  138.0 26.6 %collective-permute-start.8 = (f32[128,128]{1,0:T(8,128)}, f32[128,128]{1,0:T(8,128)}, u32[]{:S(2)}, u32[]{:S(2)}) collective-permute-start(f32[128,128]{1,0:T(8,128)} %get-tuple-element.205), channel_id=1, source_target_pairs={{0,7},{1,0},{2,1},{3,2},{4,3},{5,4},{6,5},{7,6},{8,15},{9,8},{10,9... | collective-permute-start | bytes 196616 | tf_op jit(solution)/shard_map/ppermute | solution.py:19
  138.0 25.4 %collective-permute-start.9 = (f32[128,128]{1,0:T(8,128)}, f32[128,128]{1,0:T(8,128)}, u32[]{:S(2)}, u32[]{:S(2)}) collective-permute-start(f32[128,128]{1,0:T(8,128)} %get-tuple-element.206), channel_id=1, source_target_pairs={{0,1},{1,2},{2,3},{3,4},{4,5},{5,6},{6,7},{7,0},{8,9},{9,10},{10,1... | collective-permute-start | bytes 196616 | tf_op jit(solution)/shard_map/ppermute | solution.py:19
  146.1 15.4 %copy-start.13 = (f32[1,6144]{1,0:T(1,128)S(1)}, f32[1,6144]{1,0:T(1,128)}, u32[]{:S(2)}) copy-start(f32[1,6144]{1,0:T(1,128)} %get-tuple-element.182) | copy-start | bytes 73732
  151.1 13.5 %copy-start.34 = (s32[128]{0:T(128)S(1)}, s32[128]{0:T(128)}, u32[]{:S(2)}) copy-start(s32[128]{0:T(128)} %copy-done.32) | copy-start | bytes 1540
  151.2 24.2 %copy-start.7 = (bf16[1,384,128]{2,1,0:T(8,128)(2,1)S(1)}, bf16[1,384,128]{2,1,0:T(8,128)(2,1)}, u32[]{:S(2)}) copy-start(bf16[1,384,128]{2,1,0:T(8,128)(2,1)} %get-tuple-element.210) | copy-start | bytes 294916
  165.9 2.1 collective-permute-start.10
  167.7 7.2 %collective-permute-start.11 = (f32[64,128]{1,0:T(8,128)S(1)}, f32[64,128]{1,0:T(8,128)S(1)}, u32[]{:S(2)}, u32[]{:S(2)}) collective-permute-start(f32[64,128]{1,0:T(8,128)S(1)} %get-tuple-element.224), channel_id=1, source_target_pairs={{0,8},{8,16},{16,24},{24,32},{32,40},{40,48},{48,56},{56,64},{64,7... | collective-permute-start | bytes 98312 | tf_op jit(solution)/shard_map/ppermute | solution.py:19
  213.6 17.0 %collective-permute-start.16 = (f32[3,128]{1,0:T(4,128)S(1)}, f32[3,128]{1,0:T(4,128)S(1)}, u32[]{:S(2)}, u32[]{:S(2)}) collective-permute-start(f32[3,128]{1,0:T(4,128)S(1)} %get-tuple-element.238), channel_id=1, source_target_pairs={{0,7},{1,0},{2,1},{3,2},{4,3},{5,4},{6,5},{7,6},{8,15},{9,8},{10,9... | collective-permute-start | bytes 4616 | tf_op jit(solution)/shard_map/ppermute | solution.py:19
  213.7 16.7 %collective-permute-start.17 = (f32[3,128]{1,0:T(4,128)S(1)}, f32[3,128]{1,0:T(4,128)S(1)}, u32[]{:S(2)}, u32[]{:S(2)}) collective-permute-start(f32[3,128]{1,0:T(4,128)S(1)} %get-tuple-element.239), channel_id=1, source_target_pairs={{0,1},{1,2},{2,3},{3,4},{4,5},{5,6},{6,7},{7,0},{8,9},{9,10},{10,1... | collective-permute-start | bytes 4616 | tf_op jit(solution)/shard_map/ppermute | solution.py:19
  222.3 9.7 %collective-permute-start.12 = (f32[3,128]{1,0:T(4,128)S(1)}, f32[3,128]{1,0:T(4,128)S(1)}, u32[]{:S(2)}, u32[]{:S(2)}) collective-permute-start(f32[3,128]{1,0:T(4,128)S(1)} %get-tuple-element.236), channel_id=1, source_target_pairs={{0,7},{1,0},{2,1},{3,2},{4,3},{5,4},{6,5},{7,6},{8,15},{9,8},{10,9... | collective-permute-start | bytes 4616 | tf_op jit(solution)/shard_map/ppermute | solution.py:19
  222.4 9.3 %collective-permute-start.13 = (f32[3,128]{1,0:T(4,128)S(1)}, f32[3,128]{1,0:T(4,128)S(1)}, u32[]{:S(2)}, u32[]{:S(2)}) collective-permute-start(f32[3,128]{1,0:T(4,128)S(1)} %get-tuple-element.237), channel_id=1, source_target_pairs={{0,1},{1,2},{2,3},{3,4},{4,5},{5,6},{6,7},{7,0},{8,9},{9,10},{10,1... | collective-permute-start | bytes 4616 | tf_op jit(solution)/shard_map/ppermute | solution.py:19
  230.9 6.3 %collective-permute-start.18 = (f32[3,64]{1,0:T(4,128)S(1)}, f32[3,64]{1,0:T(4,128)S(1)}, u32[]{:S(2)}, u32[]{:S(2)}) collective-permute-start(f32[3,64]{1,0:T(4,128)S(1)} %get-tuple-element.242), channel_id=1, source_target_pairs={{0,248},{8,0},{16,8},{24,16},{32,24},{40,32},{48,40},{56,48},{64,5... | collective-permute-start | bytes 2312 | tf_op jit(solution)/shard_map/ppermute | solution.py:19
  231.0 13.4 %collective-permute-start.19 = (f32[3,64]{1,0:T(4,128)S(1)}, f32[3,64]{1,0:T(4,128)S(1)}, u32[]{:S(2)}, u32[]{:S(2)}) collective-permute-start(f32[3,64]{1,0:T(4,128)S(1)} %get-tuple-element.243), channel_id=1, source_target_pairs={{0,8},{8,16},{16,24},{24,32},{32,40},{40,48},{48,56},{56,64},{64,7... | collective-permute-start | bytes 2312 | tf_op jit(solution)/shard_map/ppermute | solution.py:19
  232.2 6.3 %collective-permute-start.14 = (f32[3,64]{1,0:T(4,128)S(1)}, f32[3,64]{1,0:T(4,128)S(1)}, u32[]{:S(2)}, u32[]{:S(2)}) collective-permute-start(f32[3,64]{1,0:T(4,128)S(1)} %get-tuple-element.240), channel_id=1, source_target_pairs={{0,248},{8,0},{16,8},{24,16},{32,24},{40,32},{48,40},{56,48},{64,5... | collective-permute-start | bytes 2312 | tf_op jit(solution)/shard_map/ppermute | solution.py:19
  237.2 6.9 %collective-permute-start.15 = (f32[3,64]{1,0:T(4,128)S(1)}, f32[3,64]{1,0:T(4,128)S(1)}, u32[]{:S(2)}, u32[]{:S(2)}) collective-permute-start(f32[3,64]{1,0:T(4,128)S(1)} %get-tuple-element.241), channel_id=1, source_target_pairs={{0,8},{8,16},{16,24},{24,32},{32,40},{40,48},{48,56},{56,64},{64,7... | collective-permute-start | bytes 2312 | tf_op jit(solution)/shard_map/ppermute | solution.py:19
  (27 other events, 190.0 us)
where the time goes:
time: 250 us; the launch traced here: 245 us
  matrix products  102 us (41%)
  starting transfers between devices  51.1 us (20%)
  local copies, waits for them, and re-layouts  42 us (17%)
  waiting for transfers between devices  31 us (12%)
  other arithmetic  16.9 us (7%)
    ppermute x20, starting transfers between devices, from_behind(): return lax.ppermute(value, axis, pairs)  51.1 us
    ppermute x20, waiting for transfers between devices, from_behind(): return lax.ppermute(value, axis, pairs)  31 us
    gather x2, local copies, waits for them, and re-layouts, body(): jnp.take(pos_ext, nbr, axis=1)  17.3 us
    dot_general x6, matrix products, pick_rows(): return jnp.dot(chosen, table, preferred_element_type=jnp.float32)  13.4 us
    dot_general x2, matrix products, one_block(): jnp.dot(chosen.astype(jnp.bfloat16), h_ext, preferred_element_type=jnp.fl...  12.9 us
    dot_general x1, matrix products, one_block(): jnp.einsum('en,ec->nc', chosen, grad_msg * radial * live_b[:, None], prec...  10.8 us
    dot_general x2, matrix products, one_block(): radial = jnp.einsum('be,bc->ec', basis, weights, precision=HIGH)  10.3 us
    dot_general x2, matrix products, one_block(): jnp.einsum('lnk,nlc->nkc', harm3, grad_b, precision=HIGH).reshape(-1, width)  10.2 us
  transfers between devices with their start and end apart: 20, of which 9 were waited for; matrix products, arithmetic and copies ran while one was open for 14% of the time, Pallas kernels for 0%

commit v1 on v0

v1 whole, which is shorter than its diff:
```python
import functools
import math

import jax
import jax.numpy as jnp
from jax import lax
from jax.experimental import pallas as pl
from jax.experimental.pallas import tpu as pltpu
from jax.sharding import PartitionSpec as P

F32 = jnp.float32
BF16 = jnp.bfloat16
I32 = jnp.int32
MESH = pl.DeviceIdType.MESH

ATOMS = 128
SLOTS = 48
GROUP = 8
CHUNKS = ATOMS // GROUP
EDGES = GROUP * SLOTS
WIDTH = 128
EXT = 512
NB = 8
BOX = 8.0
SCALE = 0.25
SIDES = ((1, 0), (-1, 0), (0, 1), (0, -1), (1, 1), (1, -1), (-1, 1), (-1, -1))
R3, R5, R15 = math.sqrt(3.0), math.sqrt(5.0), math.sqrt(15.0)


def mm(a, b):
    return lax.dot_general(a, b, (((1,), (0,)), ((), ())), preferred_element_type=F32)


def nt(a, b):
    return lax.dot_general(a, b, (((1,), (1,)), ((), ())), preferred_element_type=F32)


def iota(shape, axis):
    return lax.broadcasted_iota(I32, shape, axis)


def split(value):
    high = value.astype(BF16).astype(F32)
    return high, value - high


def onehot(index, total):
    shape = (total, index.shape[1])
    return jnp.where(iota(shape, 0) == index, 1.0, 0.0).astype(BF16)


def lanes_take(row, index):
    return jnp.take_along_axis(jnp.broadcast_to(row, index.shape), index, axis=1)


def kernel(
    remote,
    pos_ref, spc_ref, nbr_ref, cnt_ref, sx_ref, sy_ref, emb_ref, rw_ref, uw_ref, ow_ref,
    en_ref, fo_ref,
    geo_out, geo_x, geo_in, geo_xin,
    h_sec, h_own, h_piece,
    g_sec, g_own, g_piece,
    p_out, p_piece, p_own, p_pin,
    nbr_d, spc_d, vec_d, harm_t, hot, hmat, hlow, basis, rad1, rad2, gat1, gat2, gms,
    amps1, amps2, gamps, z1_ref, gext, gharm, ohx, ohxt, ohy, ohyt, grel,
    send_sem, recv_sem,
):
    if remote:
        nx, ny = lax.axis_size("gx"), lax.axis_size("gy")
        me_x, me_y = lax.axis_index("gx"), lax.axis_index("gy")

        def place(side):
            return (lax.rem(me_x + side[0] + nx, nx), lax.rem(me_y + side[1] + ny, ny))

        barrier = pltpu.get_barrier_semaphore()
        for side in SIDES:
            pl.semaphore_signal(barrier, inc=1, device_id=place(side), device_id_type=MESH)

    def exchange(phase, parts):
        copies = []
        for number, side in enumerate(SIDES):
            src, dst = parts(side)
            if remote:
                copy = pltpu.make_async_remote_copy(
                    src_ref=src, dst_ref=dst,
                    send_sem=send_sem.at[phase, number], recv_sem=recv_sem.at[phase, number],
                    device_id=place(side), device_id_type=MESH,
                )
            else:
                copy = pltpu.make_async_copy(src, dst, recv_sem.at[phase, number])
            copy.start()
            copies.append(copy)
        return copies

    def finish(copies):
        for copy in copies:
            copy.wait()

    sx = jnp.concatenate([sx_ref[0:1, :], sx_ref[1:2, :]], axis=1)
    sel = jnp.where(iota((ATOMS, 128), 0) == sx, 1.0, 0.0)
    ohx[...] = sel.astype(BF16)
    ohxt[...] = sel.T.astype(BF16)

    spc = spc_ref[...].astype(F32)
    pos = pos_ref[...].astype(F32)
    zero = jnp.zeros((1, 128), F32)
    geo = jnp.concatenate([pos, spc, zero, zero, zero, zero], axis=0)
    sy = sy_ref[...].astype(F32)
    geo_out[0] = jnp.concatenate([pos, spc, sy[1:2], zero, zero, zero], axis=0)
    geo_out[1] = jnp.concatenate([pos, spc, sy[0:1], zero, zero, zero], axis=0)
    geo_x[...] = mm(geo.astype(BF16), ohx[...])

    if remote:
        pl.semaphore_wait(barrier, len(SIDES))

    def geo_parts(side):
        dx, dy = side
        if dx == 0:
            return geo_out.at[(1 + dy) // 2], geo_in.at[1 - dy]
        return geo_x, geo_xin.at[1 - dy, (1 - dx) // 2]

    copies = exchange(0, geo_parts)

    nbr_d[...] = jnp.concatenate(
        [nbr_ref[pl.ds(a, CHUNKS, stride=GROUP), :] for a in range(GROUP)], axis=1
    )

    def build(g, carry):
        hot[g] = onehot(nbr_d[pl.ds(g, 1), :], EXT)
        return carry

    lax.fori_loop(0, CHUNKS, build, 0)

    lane = iota((CHUNKS, EDGES), 1)
    of_lane = jnp.zeros((CHUNKS, EDGES), I32)
    for a in range(1, GROUP):
        of_lane += (lane >= a * SLOTS).astype(I32)
    slot = lane - of_lane * SLOTS
    atom = iota((CHUNKS, EDGES), 0) * GROUP + of_lane
    mask = of_lane[:GROUP] == iota((GROUP, EDGES), 0)

    embed_t = emb_ref[...].astype(F32).T.astype(BF16)
    w_t = []
    for t in range(2):
        high, low = split(rw_ref[t])
        w_t.append(
            jnp.concatenate([high, high, low, jnp.zeros_like(high)], axis=0).T.astype(BF16)
        )
    w_rows = []
    for t in range(2):
        w_rows.append(jnp.concatenate(split(rw_ref[t]), axis=0).astype(BF16))

    finish(copies)

    def section(j):
        own = geo if j == 0 else geo_in[1 + j]
        keep = iota((8, 128), 1) < 64
        row = iota((8, 128), 0)
        got = jnp.where(keep, geo_xin[1 + j, 0], geo_xin[1 + j, 1])
        got += jnp.where(row == 0, jnp.where(keep, -BOX, BOX), 0.0)
        return own, got

    row = iota((8, 128), 0)
    blocks = list(section(0))
    for number, j in enumerate((-1, 1)):
        own, got = section(j)
        index = own[4:5].astype(I32)
        chosen = jnp.where(iota((256, 128), 0) == index, 1.0, 0.0)
        ohy[number] = chosen.astype(BF16)
        ohyt[number] = chosen.T.astype(BF16)
        whole = jnp.concatenate([own, got], axis=1)
        whole = jnp.where(iota((8, 256), 0) < 4, whole, 0.0)
        picked = mm(whole.astype(BF16), ohy[number])
        blocks.append(picked + jnp.where(row == 1, BOX * j, 0.0))

    packed = []
    for block in blocks:
        x = ((block[0:1] + BOX) * 16.0).astype(I32)
        y = ((block[1:2] + BOX) * 16.0).astype(I32)
        zc = (block[2:3] * 16.0).astype(I32)
        packed.append(x + y * 512 + zc * 262144 + block[3:4].astype(I32) * 33554432)

    nbr = nbr_d[...]
    near = nbr & 127
    which = nbr >> 7
    far, mine, live = [], [], []
    for t in range(EDGES // 128):
        cut = slice(t * 128, (t + 1) * 128)
        value = lanes_take(packed[0], near[:, cut])
        for b in range(1, 4):
            value = jnp.where(which[:, cut] == b, lanes_take(packed[b], near[:, cut]), value)
        far.append(value)
        mine.append(lanes_take(packed[0], atom[:, cut]))
        live.append(lanes_take(cnt_ref[...], atom[:, cut]))
    far = jnp.concatenate(far, axis=1)
    mine = jnp.concatenate(mine, axis=1)
    live = jnp.where(slot < jnp.concatenate(live, axis=1), 1.0, 0.0)

    def coordinates(value):
        return value & 511, (value >> 9) & 511, (value >> 18) & 127

    rel = [
        (p - q).astype(F32) * (1.0 / 16.0)
        for p, q in zip(coordinates(far), coordinates(mine))
    ]
    square = rel[0] * rel[0] + rel[1] * rel[1] + rel[2] * rel[2] + 1.0
    dist = jnp.sqrt(square)
    inverse = 1.0 / dist
    ux, uy, uz = (r * inverse for r in rel)
    spc_d[...] = far >> 25
    for number, value in enumerate((dist, live, inverse, ux, uy, uz)):
        vec_d[number] = value
    harm = (
        R3 * ux, R3 * uy, R3 * uz, R15 * ux * uy, R15 * uy * uz,
        0.5 * R5 * (3.0 * uz * uz - 1.0), R15 * ux * uz, 0.5 * R15 * (ux * ux - uy * uy),
    )
    for number, value in enumerate(harm):
        harm_t[number] = SCALE * value

    def radial_basis(g):
        centers = 1.0 + 2.0 * iota((NB, EDGES), 0).astype(F32)
        away = vec_d[0, pl.ds(g, 1), :] - centers
        return away, jnp.exp(-0.125 * away * away) * vec_d[1, pl.ds(g, 1), :]

    def sums_of(g, message):
        high, low = split(message)
        high = high.astype(BF16)
        return nt(hmat[g], high) + nt(hlow[g], high) + nt(hmat[g], low.astype(BF16))

    def first(g, carry):
        unit = jnp.where(mask, SCALE, 0.0)
        rows = [unit]
        for m in range(8):
            rows.append(jnp.where(mask, harm_t[m, pl.ds(g, 1), :], 0.0))
        rows.append(jnp.zeros((GROUP, EDGES), F32))
        rows, fine = split(jnp.concatenate(rows, axis=0))
        hmat[g] = rows.astype(BF16)
        hlow[g] = fine.astype(BF16)
        high, low = split(radial_basis(g)[1])
        basis[g] = jnp.concatenate([high, low, high, jnp.zeros_like(high)], axis=0).astype(BF16)
        kinds = onehot(spc_d[pl.ds(g, 1), :], 16)
        gathered = mm(embed_t, kinds)
        radial = mm(w_t[0], basis[g])
        gat1[g] = gathered.astype(BF16)
        rad1[g] = radial.astype(BF16)
        sums = sums_of(g, gathered * radial)
        for m in range(9):
            amps1[m, pl.ds(pl.multiple_of(g * GROUP, GROUP), GROUP), :] = sums[
                m * GROUP : (m + 1) * GROUP
            ]
        return carry

    lax.fori_loop(0, CHUNKS, first, 0)

    def update(amps, old, t):
        one = amps[1] * amps[1] + amps[2] * amps[2] + amps[3] * amps[3]
        two = amps[4] * amps[4] + amps[5] * amps[5] + amps[6] * amps[6]
        two += amps[7] * amps[7] + amps[8] * amps[8]
        flat = jnp.concatenate([amps[0], one, two], axis=1).astype(BF16)
        z = mm(flat, uw_ref[t])
        return z, (old + z * jax.nn.sigmoid(z)).astype(BF16)

    def back(amps, z, grad, t):
        sig = jax.nn.sigmoid(z)
        grad_z = grad * (sig * (1.0 + z * (1.0 - sig)))
        grad_inv = nt(grad_z.astype(BF16), uw_ref[t])
        gamps[0] = grad_inv[:, :128]
        for m in range(1, 9):
            part = grad_inv[:, 128:256] if m < 4 else grad_inv[:, 256:]
            gamps[m] = 2.0 * amps[m] * part

    kinds_own = onehot(spc_ref[...], 16).astype(F32).T.astype(BF16)
    h0_own = mm(kinds_own, emb_ref[...])
    z1, h1 = update(amps1, h0_own, 0)
    z1_ref[...] = z1
    h_sec[1, 0:128] = h1
    h_own[...] = h1
    h_piece[...] = mm(ohxt[...], h1).astype(BF16)

    def h_parts(side):
        dx, dy = side
        if dx == 0:
            return h_own, h_sec.at[1 - dy, pl.ds(0, 128)]
        if dx == 1:
            return h_piece.at[pl.ds(0, 64)], h_sec.at[1 - dy, pl.ds(128, 64)]
        return h_piece.at[pl.ds(64, 64)], h_sec.at[1 - dy, pl.ds(192, 64)]

    copies = exchange(1, h_parts)

    def second_radial(g, carry):
        rad2[g] = mm(w_t[1], basis[g])
        return carry

    lax.fori_loop(0, CHUNKS, second_radial, 0)
    own_t = h1.astype(F32).T
    finish(copies)

    got_t = h_sec[1, 128:256].astype(F32).T
    low_t = mm(ohyt[0], h_sec[0]).T
    high_t = mm(ohyt[1], h_sec[2]).T
    h_t = jnp.concatenate([own_t, got_t, low_t, high_t], axis=1).astype(BF16)

    def second(g, carry):
        gathered = mm(h_t, hot[g])
        gat2[g] = gathered.astype(BF16)
        sums = sums_of(g, gathered * rad2[g])
        for m in range(9):
            amps2[m, pl.ds(pl.multiple_of(g * GROUP, GROUP), GROUP), :] = sums[
                m * GROUP : (m + 1) * GROUP
            ]
        return carry

    lax.fori_loop(0, CHUNKS, second, 0)
    z2, h2 = update(amps2, h1.astype(F32), 1)
    out_w = ow_ref[...]
    high, rest = split(out_w)
    mid, low = split(rest)
    readout = jnp.concatenate([high, mid, low, jnp.zeros((5, 128), F32)], axis=0).astype(BF16)
    parts = nt(readout, h2)
    en_ref[...] = parts[0:1] + parts[1:2] + parts[2:3]
    back(amps2, z2, out_w, 1)

    gext[...] = jnp.zeros_like(gext)

    def chunk_rows(g):
        at = pl.ds(pl.multiple_of(g * GROUP, GROUP), GROUP)
        rows = [gamps[m, at, :] for m in range(9)] + [jnp.zeros((GROUP, 128), F32)]
        return jnp.concatenate(rows, axis=0)

    def features(g, carry):
        grad = mm(chunk_rows(g).T.astype(BF16), hmat[g])
        gms[g] = grad.astype(BF16)
        rows = (grad * rad2[g]).astype(BF16)
        gext[...] += nt(hot[g], rows)
        return carry

    lax.fori_loop(0, CHUNKS, features, 0)

    for number, start in ((0, 256), (1, 384)):
        g_sec[2 * number] = mm(ohy[number], gext[start : start + 128].astype(BF16)).astype(BF16)
    g_sec[1, 128:256] = gext[128:256].astype(BF16)

    def g_parts(side):
        dx, dy = side
        if dx == 0:
            return g_sec.at[1 + dy, pl.ds(0, 128)], g_own.at[(1 - dy) // 2]
        if dx == -1:
            return g_sec.at[1 + dy, pl.ds(128, 64)], g_piece.at[1 - dy, pl.ds(0, 64)]
        return g_sec.at[1 + dy, pl.ds(192, 64)], g_piece.at[1 - dy, pl.ds(64, 64)]

    copies = exchange(2, g_parts)

    def adjoint(g, grad, gathered, radial, t):
        message = (gathered * radial).astype(BF16)
        wide = mm(chunk_rows(g).astype(BF16), message)
        rows = []
        for m in range(1, 9):
            part = jnp.where(mask, wide[m * GROUP : (m + 1) * GROUP], 0.0)
            rows.append(jnp.sum(part, axis=0, keepdims=True))
        two = mm(w_rows[t], (grad * gathered).astype(BF16))
        away, value = radial_basis(g)
        slope = (two[0:NB] + two[NB:]) * (-0.25 * away * value)
        rows.append(jnp.sum(slope, axis=0, keepdims=True))
        return rows

    def geometry_two(g, carry):
        rows = adjoint(
            g, gms[g].astype(F32), gat2[g].astype(F32), rad2[g], 1
        )
        for number, value in enumerate(rows):
            gharm[number, pl.ds(g, 1), :] = value
        return carry

    lax.fori_loop(0, CHUNKS, geometry_two, 0)
    finish(copies)

    grad_h1 = gext[0:128] + out_w + g_own[0].astype(F32) + g_own[1].astype(F32)
    piece = g_piece[0].astype(F32) + g_piece[1].astype(F32) + g_piece[2].astype(F32)
    grad_h1 += mm(ohx[...], piece.astype(BF16))
    back(amps1, z1_ref[...], grad_h1, 0)

    def geometry_one(g, carry):
        grad = mm(chunk_rows(g).T.astype(BF16), hmat[g])
        rows = adjoint(g, grad, gat1[g].astype(F32), rad1[g].astype(F32), 0)
        for number, value in enumerate(rows):
            gharm[number, pl.ds(g, 1), :] += value
        return carry

    lax.fori_loop(0, CHUNKS, geometry_one, 0)

    inv, vx, vy, vz = (vec_d[n] for n in range(2, 6))
    g1, g2, g3, g4, g5, g6, g7, g8 = (SCALE * gharm[n] for n in range(8))
    gx = R3 * g1 + R15 * (vy * g4 + vz * g7 + vx * g8)
    gy = R3 * g2 + R15 * (vx * g4 + vz * g5 - vy * g8)
    gz = R3 * g3 + R15 * (vy * g5 + vx * g7) + 3.0 * R5 * vz * g6
    along = gharm[8] - inv * (gx * vx + gy * vy + gz * vz)
    wide_rows = []
    for number, (grad, unit) in enumerate(((gx, vx), (gy, vy), (gz, vz))):
        high, low = split(grad * inv + unit * along)
        grel[number] = high
        grel[3 + number] = low
        wide_rows += [high, low]
    grel[6] = jnp.zeros((CHUNKS, EDGES), F32)
    grel[7] = jnp.zeros((CHUNKS, EDGES), F32)

    lane_atom = jnp.where(iota((ATOMS, EDGES), 0) % GROUP == of_lane[0:1], 1.0, 0.0).astype(BF16)
    sums = nt(jnp.concatenate(wide_rows, axis=0).astype(BF16), lane_atom)
    here = iota((CHUNKS, 128), 1) // GROUP == iota((CHUNKS, 128), 0)
    own_rows = []
    for number in range(3):
        both = sums[32 * number : 32 * number + 16] + sums[32 * number + 16 : 32 * number + 32]
        own_rows.append(jnp.sum(jnp.where(here, both, 0.0), axis=0, keepdims=True))

    def scatter(g, total):
        rows = jnp.concatenate([grel[n, pl.ds(g, 1), :] for n in range(8)], axis=0)
        return total + nt(rows.astype(BF16), hot[g])

    total = lax.fori_loop(0, CHUNKS, scatter, jnp.zeros((8, EXT), F32))
    total = total[0:3] + total[3:6]
    own_rows = jnp.concatenate(own_rows, axis=0)

    def six(value):
        high, low = split(value)
        return jnp.concatenate([high, low, jnp.zeros((2, value.shape[1]), F32)], axis=0).astype(BF16)

    def three(value):
        return value[0:3] + value[3:6]

    pad = jnp.zeros((5, 128), F32)
    for number, start in ((0, 256), (1, 384)):
        spread = three(nt(six(total[:, start : start + 128]), ohy[number]))
        p_out[number] = jnp.concatenate([spread[:, 0:128], pad], axis=0)
        p_piece[2 * number] = jnp.concatenate([spread[:, 128:256], pad], axis=0)
    p_piece[1] = jnp.concatenate([total[:, 128:256], pad], axis=0)

    def p_parts(side):
        dx, dy = side
        if dx == 0:
            return p_out.at[(1 + dy) // 2], p_own.at[(1 - dy) // 2]
        return p_piece.at[1 + dy], p_pin.at[1 - dy, (1 + dx) // 2]

    finish(exchange(3, p_parts))
    up = p_pin[0, 0] + p_pin[1, 0] + p_pin[2, 0]
    down = p_pin[0, 1] + p_pin[1, 1] + p_pin[2, 1]
    piece = jnp.where(iota((8, 128), 1) < 64, up, down)[0:3]
    result = total[:, 0:128] - own_rows + p_own[0][0:3] + p_own[1][0:3]
    result += three(nt(six(piece), ohx[...]))
    fo_ref[...] = -result


def body(remote, positions, species, neighbours, counts, send_x, send_y, embed, radial_w, update_w, out_w):
    embed = jnp.pad(embed, ((0, 16 - embed.shape[0]), (0, 0)))
    vmem = pl.BlockSpec(memory_space=pltpu.VMEM)
    chunked = (CHUNKS, 128, EDGES)
    scratch = [
        pltpu.VMEM((2, 8, 128), F32),
        pltpu.VMEM((8, 128), F32),
        pltpu.VMEM((3, 8, 128), F32),
        pltpu.VMEM((3, 2, 8, 128), F32),
        pltpu.VMEM((3, 256, 128), BF16),
        pltpu.VMEM((128, 128), BF16),
        pltpu.VMEM((128, 128), BF16),
        pltpu.VMEM((3, 256, 128), BF16),
        pltpu.VMEM((2, 128, 128), BF16),
        pltpu.VMEM((3, 128, 128), BF16),
        pltpu.VMEM((2, 8, 128), F32),
        pltpu.VMEM((3, 8, 128), F32),
        pltpu.VMEM((2, 8, 128), F32),
        pltpu.VMEM((3, 2, 8, 128), F32),
        pltpu.VMEM((CHUNKS, EDGES), I32),
        pltpu.VMEM((CHUNKS, EDGES), I32),
        pltpu.VMEM((6, CHUNKS, EDGES), F32),
        pltpu.VMEM((8, CHUNKS, EDGES), F32),
        pltpu.VMEM((CHUNKS, EXT, EDGES), BF16),
        pltpu.VMEM((CHUNKS, 80, EDGES), BF16),
        pltpu.VMEM((CHUNKS, 80, EDGES), BF16),
        pltpu.VMEM((CHUNKS, 32, EDGES), BF16),
        pltpu.VMEM(chunked, BF16),
        pltpu.VMEM(chunked, F32),
        pltpu.VMEM(chunked, BF16),
        pltpu.VMEM(chunked, BF16),
        pltpu.VMEM(chunked, BF16),
        pltpu.VMEM((9, 128, 128), F32),
        pltpu.VMEM((9, 128, 128), F32),
        pltpu.VMEM((9, 128, 128), F32),
        pltpu.VMEM((128, 128), F32),
        pltpu.VMEM((EXT, 128), F32),
        pltpu.VMEM((9, CHUNKS, EDGES), F32),
        pltpu.VMEM((128, 128), BF16),
        pltpu.VMEM((128, 128), BF16),
        pltpu.VMEM((2, 256, 128), BF16),
        pltpu.VMEM((2, 128, 256), BF16),
        pltpu.VMEM((8, CHUNKS, EDGES), F32),
        pltpu.SemaphoreType.DMA((4, 8)),
        pltpu.SemaphoreType.DMA((4, 8)),
    ]
    energy, forces = pl.pallas_call(
        functools.partial(kernel, remote),
        out_shape=(
            jax.ShapeDtypeStruct((1, ATOMS), F32),
            jax.ShapeDtypeStruct((3, ATOMS), F32),
        ),
        in_specs=[vmem] * 10,
        out_specs=(vmem, vmem),
        scratch_shapes=scratch,
        compiler_params=pltpu.CompilerParams(
            collective_id=0 if remote else None,
            has_side_effects=remote,
            vmem_limit_bytes=48 * 1024 * 1024,
        ),
    )(
        positions,
        species.reshape(1, ATOMS),
        neighbours,
        counts.reshape(1, ATOMS),
        send_x.reshape(2, 64),
        send_y.reshape(2, 128),
        embed,
        radial_w,
        update_w,
        out_w.reshape(1, WIDTH),
    )
    return energy.reshape(ATOMS), forces


def solution(mesh):
    return jax.shard_map(
        functools.partial(body, True),
        mesh=mesh,
        in_specs=(
            P(None, ("gx", "gy")),
            P(("gx", "gy")),
            P(("gx", "gy"), None),
            P(("gx", "gy")),
            P(("gx", "gy"), None, None),
            P(("gx", "gy"), None, None),
            P(),
            P(),
            P(),
            P(),
        ),
        out_specs=(P(("gx", "gy")), P(None, ("gx", "gy"))),
        check_vma=False,
    )
```

time: 250 us -> 77.7 us (0.31)
  the two profiles are of different devices: /device:TPU:24 before, /device:TPU:1 now
where the time goes in v1:
time: 77.7 us; the launch traced here: 77.3 us
  Pallas kernels  73 us (94%)
  local copies, waits for them, and re-layouts  3.61 us (5%)
    pallas_call x1, Pallas kernels, body(): pl.pallas_call(functools.partial(kernel, remote), out_shape=(jax.ShapeDty...  73 us
    unnamed x21, local copies, waits for them, and re-layouts  3.6 us

profile of v1, /device:TPU:1, one launch (start us, length us, event | category | flops | bytes accessed | tf_op | source)
XLA Modules:
  0.0 77.3 jit_solution(997179735328245638)
XLA Ops:
  0.6 0.0 copy-start.8
  0.6 0.7 copy-done.8
  1.3 0.0 copy-start.1
  1.3 0.0 copy-start.2
  1.3 0.0 copy-start.3
  1.3 0.0 copy-start.4
  1.4 0.0 copy-start.5
  1.4 0.0 copy-start.6
  1.4 0.0 copy-start.7
  1.4 0.9 %copy.12.nbr_ref = s32[128,48]{1,0:T(8,128)S(1)} copy(s32[128,48]{0,1:T(8,128)} %param.12) | data formatting | bytes 49152 | tf_op args[2]
  2.3 0.0 copy-done.1
  2.3 0.0 copy-done.2
  2.3 0.0 copy-done.3
  2.3 0.0 copy-done.4
  2.3 0.0 copy-done.5
  2.3 0.0 copy-done.6
  2.3 0.0 copy-done.7
  2.3 0.0 copy-start
  2.3 0.9 %copy-done = bf16[2,384,128]{2,1,0:T(8,128)(2,1)S(1)} copy-done((bf16[2,384,128]{2,1,0:T(8,128)(2,1)S(1)}, bf16[2,384,128]{2,1,0:T(8,128)(2,1)}, u32[]{:S(2)}) %copy-start) | copy-done | bytes 196632
  3.3 73.0 %shard_map.113 = (f32[1,128]{1,0:T(1,128)S(1)}, f32[3,128]{1,0:T(4,128)S(1)}) custom-call(bf16[3,128]{1,0:T(4,128)(2,1)S(1)} %copy-done.2, s32[1,128]{1,0:T(1,128)S(1)} %bitcast.8, s32[128,48]{1,0:T(8,128)S(1)} %copy.12.nbr_ref, s32[1,128]{1,0:T(1,128)S(1)} %bitcast.9, s32[2,64]{1,0:T(2,128)S(1)} %bitcast.6, s32[2,128]{1,0:T(2,128)S(1)} %bitcast.7, ...), custom_call_target="tpu_custom_call" | custom-call | tf_op jit(solution)/shard_map/pallas_call | solution.py:497
  76.3 0.5 copy.15
  76.8 0.6 copy.16
  (1 shorter events, 0.0 us)
Async XLA Ops:
  0.6 0.7 copy-start.8
  1.3 0.9 %copy-start.1 = (f32[2,8,128]{2,1,0:T(8,128)S(1)}, f32[2,8,128]{2,1,0:T(8,128)}, u32[]{:S(2)}) copy-start(f32[2,8,128]{2,1,0:T(8,128)} %rw_ref.1) | copy-start | bytes 24580
  1.3 1.0 %copy-start.2 = (bf16[3,128]{1,0:T(4,128)(2,1)S(1)}, bf16[3,128]{1,0:T(4,128)(2,1)}, u32[]{:S(2)}) copy-start(bf16[3,128]{1,0:T(4,128)(2,1)} %pos_ref.1) | copy-start | bytes 2308
  1.3 1.0 %copy-start.3 = (s32[1,2,64]{2,1,0:T(2,128)S(1)}, s32[1,2,64]{2,1,0:T(2,128)}, u32[]{:S(2)}) copy-start(s32[1,2,64]{2,1,0:T(2,128)} %param.14) | copy-start | bytes 1540
  1.3 1.0 %copy-start.4 = (s32[1,2,128]{2,1,0:T(2,128)S(1)}, s32[1,2,128]{2,1,0:T(2,128)}, u32[]{:S(2)}) copy-start(s32[1,2,128]{2,1,0:T(2,128)} %param.15) | copy-start | bytes 3076
  1.4 1.0 %copy-start.5 = (s32[128]{0:T(128)S(1)}, s32[128]{0:T(128)}, u32[]{:S(2)}) copy-start(s32[128]{0:T(128)} %param.11) | copy-start | bytes 1540
  1.4 0.9 %copy-start.6 = (s32[128]{0:T(128)S(1)}, s32[128]{0:T(128)}, u32[]{:S(2)}) copy-start(s32[128]{0:T(128)} %param.13) | copy-start | bytes 1540
  1.4 0.9 %copy-start.7 = (f32[128]{0:T(128)S(1)}, f32[128]{0:T(128)}, u32[]{:S(2)}) copy-start(f32[128]{0:T(128)} %param.19) | copy-start | bytes 1540
  2.3 0.9 %copy-start = (bf16[2,384,128]{2,1,0:T(8,128)(2,1)S(1)}, bf16[2,384,128]{2,1,0:T(8,128)(2,1)}, u32[]{:S(2)}) copy-start(bf16[2,384,128]{2,1,0:T(8,128)(2,1)} %uw_ref.1) | copy-start | bytes 589828

commit v2 on v1

--- a/solution.py
+++ b/solution.py
@@ -17,6 +17,7 @@
 SLOTS = 48
 GROUP = 8
 CHUNKS = ATOMS // GROUP
+PAIRS = CHUNKS // 2
 EDGES = GROUP * SLOTS
 WIDTH = 128
 EXT = 512
@@ -55,15 +56,15 @@
 
 def kernel(
     remote,
-    pos_ref, spc_ref, nbr_ref, cnt_ref, sx_ref, sy_ref, emb_ref, rw_ref, uw_ref, ow_ref,
+    pos_ref, spc_ref, nbr_ref, cnt_ref, sx_ref, sy_ref, emb_ref, rw_ref, uw_hbm, ow_ref,
     en_ref, fo_ref,
     geo_out, geo_x, geo_in, geo_xin,
     h_sec, h_own, h_piece,
     g_sec, g_own, g_piece,
     p_out, p_piece, p_own, p_pin,
-    nbr_d, spc_d, vec_d, harm_t, hot, hmat, hlow, basis, rad1, rad2, gat1, gat2, gms,
-    amps1, amps2, gamps, z1_ref, gext, gharm, ohx, ohxt, ohy, ohyt, grel,
-    send_sem, recv_sem,
+    nbr_t, nbr_d, spc_d, vec_d, harm_t, hot, hmat, hlow, basis, phi, rad2, gat2, gms, rows_t,
+    kinds_amps, amps1, amps2, gamps, z1_ref, gext, gharm, ohx, ohxt, ohy, ohyt,
+    uw_ref, uw_sem, send_sem, recv_sem,
 ):
     if remote:
         nx, ny = lax.axis_size("gx"), lax.axis_size("gy")
@@ -96,6 +97,9 @@
         for copy in copies:
             copy.wait()
 
+    weights = pltpu.make_async_copy(uw_hbm, uw_ref, uw_sem)
+    weights.start()
+
     sx = jnp.concatenate([sx_ref[0:1, :], sx_ref[1:2, :]], axis=1)
     sel = jnp.where(iota((ATOMS, 128), 0) == sx, 1.0, 0.0)
     ohx[...] = sel.astype(BF16)
@@ -121,15 +125,25 @@
 
     copies = exchange(0, geo_parts)
 
+    nbr_t[...] = nbr_ref[...].T
     nbr_d[...] = jnp.concatenate(
-        [nbr_ref[pl.ds(a, CHUNKS, stride=GROUP), :] for a in range(GROUP)], axis=1
+        [nbr_t[pl.ds(a, CHUNKS, stride=GROUP), :] for a in range(GROUP)], axis=1
     )
 
+    def lanes(g, count=1):
+        return pl.ds(pl.multiple_of(g * (count * EDGES), 128), count * EDGES)
+
     def build(g, carry):
-        hot[g] = onehot(nbr_d[pl.ds(g, 1), :], EXT)
-        return carry
-
-    lax.fori_loop(0, CHUNKS, build, 0)
+        index = jnp.broadcast_to(nbr_d[pl.ds(g, 1), :], (16, EDGES)).astype(jnp.int16)
+        one, none = jnp.ones((16, EDGES), BF16), jnp.zeros((16, EDGES), BF16)
+        first_rows = iota((16, EDGES), 0).astype(jnp.int16)
+        for block in range(EXT // 16):
+            hot[16 * block : 16 * block + 16, lanes(g)] = jnp.where(
+                index - jnp.int16(16 * block) == first_rows, one, none
+            )
+        return carry
+
+    lax.fori_loop(0, CHUNKS, build, 0, unroll=8)
 
     lane = iota((CHUNKS, EDGES), 1)
     of_lane = jnp.zeros((CHUNKS, EDGES), I32)
@@ -139,16 +153,13 @@
     atom = iota((CHUNKS, EDGES), 0) * GROUP + of_lane
     mask = of_lane[:GROUP] == iota((GROUP, EDGES), 0)
 
-    embed_t = emb_ref[...].astype(F32).T.astype(BF16)
-    w_t = []
-    for t in range(2):
-        high, low = split(rw_ref[t])
-        w_t.append(
-            jnp.concatenate([high, high, low, jnp.zeros_like(high)], axis=0).T.astype(BF16)
-        )
-    w_rows = []
-    for t in range(2):
-        w_rows.append(jnp.concatenate(split(rw_ref[t]), axis=0).astype(BF16))
+    high, low = split(rw_ref[1])
+    w_t = jnp.concatenate([high, high, low, jnp.zeros_like(high)], axis=0).T.astype(BF16)
+    w_rows = jnp.concatenate([high, low], axis=0).astype(BF16)
+    embed = emb_ref[...].astype(F32)
+    species = embed.shape[0]
+    kind_w = jnp.concatenate([rw_ref[0] * embed[k : k + 1] for k in range(species)], axis=0)
+    kind_high, kind_low = (v.astype(BF16) for v in split(kind_w))
 
     finish(copies)
 
@@ -222,10 +233,14 @@
         away = vec_d[0, pl.ds(g, 1), :] - centers
         return away, jnp.exp(-0.125 * away * away) * vec_d[1, pl.ds(g, 1), :]
 
-    def sums_of(g, message):
-        high, low = split(message)
-        high = high.astype(BF16)
-        return nt(hmat[g], high) + nt(hlow[g], high) + nt(hmat[g], low.astype(BF16))
+    def sums_of(g, high, low):
+        left = jnp.concatenate([hmat[g], hlow[g], hmat[g]], axis=1)
+        return nt(left, jnp.concatenate([high, high, low], axis=1))
+
+    def store_sums(ref, g, sums):
+        at = pl.ds(pl.multiple_of(g * GROUP, GROUP), GROUP)
+        for m in range(9):
+            ref[m, at, :] = sums[m * GROUP : (m + 1) * GROUP]
 
     def first(g, carry):
         unit = jnp.where(mask, SCALE, 0.0)
@@ -238,19 +253,20 @@
         hlow[g] = fine.astype(BF16)
         high, low = split(radial_basis(g)[1])
         basis[g] = jnp.concatenate([high, low, high, jnp.zeros_like(high)], axis=0).astype(BF16)
-        kinds = onehot(spc_d[pl.ds(g, 1), :], 16)
-        gathered = mm(embed_t, kinds)
-        radial = mm(w_t[0], basis[g])
-        gat1[g] = gathered.astype(BF16)
-        rad1[g] = radial.astype(BF16)
-        sums = sums_of(g, gathered * radial)
-        for m in range(9):
-            amps1[m, pl.ds(pl.multiple_of(g * GROUP, GROUP), GROUP), :] = sums[
-                m * GROUP : (m + 1) * GROUP
-            ]
-        return carry
-
-    lax.fori_loop(0, CHUNKS, first, 0)
+        kind = spc_d[pl.ds(g, 1), :]
+        phi_high, phi_low = (
+            jnp.concatenate([jnp.where(kind == k, v, 0.0) for k in range(species)], axis=0)
+            for v in (high, low)
+        )
+        phi[g] = phi_high.astype(BF16)
+        store_sums(kinds_amps, g, sums_of(g, phi[g], phi_low.astype(BF16)))
+        return carry
+
+    lax.fori_loop(0, CHUNKS, first, 0, unroll=8)
+    for m in range(9):
+        high, low = (v.astype(BF16) for v in split(kinds_amps[m]))
+        amps1[m] = mm(high, kind_high) + mm(low, kind_high) + mm(high, kind_low)
+    weights.wait()
 
     def update(amps, old, t):
         one = amps[1] * amps[1] + amps[2] * amps[2] + amps[3] * amps[3]
@@ -270,7 +286,9 @@
             gamps[m] = 2.0 * amps[m] * part
 
     kinds_own = onehot(spc_ref[...], 16).astype(F32).T.astype(BF16)
-    h0_own = mm(kinds_own, emb_ref[...])
+    h0_own = mm(
+        kinds_own, jnp.concatenate([embed, jnp.zeros((16 - species, 128), F32)], axis=0).astype(BF16)
+    )
     z1, h1 = update(amps1, h0_own, 0)
     z1_ref[...] = z1
     h_sec[1, 0:128] = h1
@@ -288,10 +306,10 @@
     copies = exchange(1, h_parts)
 
     def second_radial(g, carry):
-        rad2[g] = mm(w_t[1], basis[g])
-        return carry
-
-    lax.fori_loop(0, CHUNKS, second_radial, 0)
+        rad2[:, lanes(g)] = mm(w_t, basis[g])
+        return carry
+
+    lax.fori_loop(0, CHUNKS, second_radial, 0, unroll=8)
     own_t = h1.astype(F32).T
     finish(copies)
 
@@ -300,17 +318,17 @@
     high_t = mm(ohyt[1], h_sec[2]).T
     h_t = jnp.concatenate([own_t, got_t, low_t, high_t], axis=1).astype(BF16)
 
-    def second(g, carry):
-        gathered = mm(h_t, hot[g])
-        gat2[g] = gathered.astype(BF16)
-        sums = sums_of(g, gathered * rad2[g])
-        for m in range(9):
-            amps2[m, pl.ds(pl.multiple_of(g * GROUP, GROUP), GROUP), :] = sums[
-                m * GROUP : (m + 1) * GROUP
-            ]
-        return carry
-
-    lax.fori_loop(0, CHUNKS, second, 0)
+    def second(p, carry):
+        gathered = mm(h_t, hot[:, lanes(p, 2)])
+        gat2[:, lanes(p, 2)] = gathered.astype(BF16)
+        for half in range(2):
+            g = 2 * p + half
+            message = gathered[:, half * EDGES : (half + 1) * EDGES] * rad2[:, lanes(g)]
+            high, low = (v.astype(BF16) for v in split(message))
+            store_sums(amps2, g, sums_of(g, high, low))
+        return carry
+
+    lax.fori_loop(0, PAIRS, second, 0, unroll=4)
     z2, h2 = update(amps2, h1.astype(F32), 1)
     out_w = ow_ref[...]
     high, rest = split(out_w)
@@ -320,21 +338,19 @@
     en_ref[...] = parts[0:1] + parts[1:2] + parts[2:3]
     back(amps2, z2, out_w, 1)
 
-    gext[...] = jnp.zeros_like(gext)
-
-    def chunk_rows(g):
+    def chunk_rows(ref, g):
         at = pl.ds(pl.multiple_of(g * GROUP, GROUP), GROUP)
-        rows = [gamps[m, at, :] for m in range(9)] + [jnp.zeros((GROUP, 128), F32)]
-        return jnp.concatenate(rows, axis=0)
+        rows = [ref[m, at, :] for m in range(9)]
+        return jnp.concatenate(rows + [jnp.zeros_like(rows[0])], axis=0)
 
     def features(g, carry):
-        grad = mm(chunk_rows(g).T.astype(BF16), hmat[g])
-        gms[g] = grad.astype(BF16)
-        rows = (grad * rad2[g]).astype(BF16)
-        gext[...] += nt(hot[g], rows)
-        return carry
-
-    lax.fori_loop(0, CHUNKS, features, 0)
+        grad = mm(chunk_rows(gamps, g).T.astype(BF16), hmat[g])
+        gms[:, lanes(g)] = grad.astype(BF16)
+        rows_t[:, lanes(g)] = (grad * rad2[:, lanes(g)]).astype(BF16)
+        return carry
+
+    lax.fori_loop(0, CHUNKS, features, 0, unroll=8)
+    gext[...] = nt(hot[...], rows_t[...])
 
     for number, start in ((0, 256), (1, 384)):
         g_sec[2 * number] = mm(ohy[number], gext[start : start + 128].astype(BF16)).astype(BF16)
@@ -350,28 +366,28 @@
 
     copies = exchange(2, g_parts)
 
-    def adjoint(g, grad, gathered, radial, t):
-        message = (gathered * radial).astype(BF16)
-        wide = mm(chunk_rows(g).astype(BF16), message)
+    def harmonic_rows(wide):
         rows = []
         for m in range(1, 9):
             part = jnp.where(mask, wide[m * GROUP : (m + 1) * GROUP], 0.0)
             rows.append(jnp.sum(part, axis=0, keepdims=True))
-        two = mm(w_rows[t], (grad * gathered).astype(BF16))
+        return rows
+
+    def distance_row(g, by_basis):
         away, value = radial_basis(g)
-        slope = (two[0:NB] + two[NB:]) * (-0.25 * away * value)
-        rows.append(jnp.sum(slope, axis=0, keepdims=True))
-        return rows
+        return jnp.sum(by_basis * (-0.25 * away * value), axis=0, keepdims=True)
 
     def geometry_two(g, carry):
-        rows = adjoint(
-            g, gms[g].astype(F32), gat2[g].astype(F32), rad2[g], 1
-        )
+        gathered = gat2[:, lanes(g)].astype(F32)
+        message = (gathered * rad2[:, lanes(g)]).astype(BF16)
+        rows = harmonic_rows(mm(chunk_rows(gamps, g).astype(BF16), message))
+        two = mm(w_rows, (gms[:, lanes(g)].astype(F32) * gathered).astype(BF16))
+        rows.append(distance_row(g, two[0:NB] + two[NB:]))
         for number, value in enumerate(rows):
             gharm[number, pl.ds(g, 1), :] = value
         return carry
 
-    lax.fori_loop(0, CHUNKS, geometry_two, 0)
+    lax.fori_loop(0, CHUNKS, geometry_two, 0, unroll=8)
     finish(copies)
 
     grad_h1 = gext[0:128] + out_w + g_own[0].astype(F32) + g_own[1].astype(F32)
@@ -379,14 +395,23 @@
     grad_h1 += mm(ohx[...], piece.astype(BF16))
     back(amps1, z1_ref[...], grad_h1, 0)
 
+    for m in range(9):
+        kinds_amps[m] = nt(gamps[m].astype(BF16), kind_high)
+
     def geometry_one(g, carry):
-        grad = mm(chunk_rows(g).T.astype(BF16), hmat[g])
-        rows = adjoint(g, grad, gat1[g].astype(F32), rad1[g].astype(F32), 0)
+        grads = chunk_rows(kinds_amps, g)
+        rows = harmonic_rows(mm(grads.astype(BF16), phi[g]))
+        by_kind = mm(grads.T.astype(BF16), hmat[g])
+        kind = spc_d[pl.ds(g, 1), :]
+        by_basis = jnp.where(kind == 0, by_kind[0:NB], 0.0)
+        for k in range(1, species):
+            by_basis += jnp.where(kind == k, by_kind[k * NB : (k + 1) * NB], 0.0)
+        rows.append(distance_row(g, by_basis))
         for number, value in enumerate(rows):
             gharm[number, pl.ds(g, 1), :] += value
         return carry
 
-    lax.fori_loop(0, CHUNKS, geometry_one, 0)
+    lax.fori_loop(0, CHUNKS, geometry_one, 0, unroll=8)
 
     inv, vx, vy, vz = (vec_d[n] for n in range(2, 6))
     g1, g2, g3, g4, g5, g6, g7, g8 = (SCALE * gharm[n] for n in range(8))
@@ -395,13 +420,8 @@
     gz = R3 * g3 + R15 * (vy * g5 + vx * g7) + 3.0 * R5 * vz * g6
     along = gharm[8] - inv * (gx * vx + gy * vy + gz * vz)
     wide_rows = []
-    for number, (grad, unit) in enumerate(((gx, vx), (gy, vy), (gz, vz))):
-        high, low = split(grad * inv + unit * along)
-        grel[number] = high
-        grel[3 + number] = low
-        wide_rows += [high, low]
-    grel[6] = jnp.zeros((CHUNKS, EDGES), F32)
-    grel[7] = jnp.zeros((CHUNKS, EDGES), F32)
+    for grad, unit in ((gx, vx), (gy, vy), (gz, vz)):
+        wide_rows += split(grad * inv + unit * along)
 
     lane_atom = jnp.where(iota((ATOMS, EDGES), 0) % GROUP == of_lane[0:1], 1.0, 0.0).astype(BF16)
     sums = nt(jnp.concatenate(wide_rows, axis=0).astype(BF16), lane_atom)
@@ -411,12 +431,20 @@
         both = sums[32 * number : 32 * number + 16] + sums[32 * number + 16 : 32 * number + 32]
         own_rows.append(jnp.sum(jnp.where(here, both, 0.0), axis=0, keepdims=True))
 
-    def scatter(g, total):
-        rows = jnp.concatenate([grel[n, pl.ds(g, 1), :] for n in range(8)], axis=0)
-        return total + nt(rows.astype(BF16), hot[g])
-
-    total = lax.fori_loop(0, CHUNKS, scatter, jnp.zeros((8, EXT), F32))
-    total = total[0:3] + total[3:6]
+    upper, lower = nbr >> 6, nbr & 63
+    left, right = [], []
+    for g in range(CHUNKS):
+        here = iota((8, EDGES), 0) == upper[g : g + 1]
+        left.append(
+            jnp.concatenate([jnp.where(here, v[g : g + 1], 0.0) for v in wide_rows], axis=0).astype(BF16)
+        )
+        right.append(onehot(lower[g : g + 1], 64))
+    both = nt(jnp.concatenate(left, axis=1), jnp.concatenate(right, axis=1))
+    coords = []
+    for number in range(3):
+        value = both[16 * number : 16 * number + 8] + both[16 * number + 8 : 16 * number + 16]
+        coords.append(jnp.concatenate([value[k : k + 1] for k in range(8)], axis=1))
+    total = jnp.concatenate(coords, axis=0)
     own_rows = jnp.concatenate(own_rows, axis=0)
 
     def six(value):
@@ -449,9 +477,9 @@
 
 
 def body(remote, positions, species, neighbours, counts, send_x, send_y, embed, radial_w, update_w, out_w):
-    embed = jnp.pad(embed, ((0, 16 - embed.shape[0]), (0, 0)))
     vmem = pl.BlockSpec(memory_space=pltpu.VMEM)
-    chunked = (CHUNKS, 128, EDGES)
+    kinds = embed.shape[0] * NB
+    whole = (128, CHUNKS * EDGES)
     scratch = [
         pltpu.VMEM((2, 8, 128), F32),
         pltpu.VMEM((8, 128), F32),
@@ -467,19 +495,21 @@
         pltpu.VMEM((3, 8, 128), F32),
         pltpu.VMEM((2, 8, 128), F32),
         pltpu.VMEM((3, 2, 8, 128), F32),
+        pltpu.VMEM((ATOMS, SLOTS), I32),
         pltpu.VMEM((CHUNKS, EDGES), I32),
         pltpu.VMEM((CHUNKS, EDGES), I32),
         pltpu.VMEM((6, CHUNKS, EDGES), F32),
         pltpu.VMEM((8, CHUNKS, EDGES), F32),
-        pltpu.VMEM((CHUNKS, EXT, EDGES), BF16),
+        pltpu.VMEM((EXT, CHUNKS * EDGES), BF16),
         pltpu.VMEM((CHUNKS, 80, EDGES), BF16),
         pltpu.VMEM((CHUNKS, 80, EDGES), BF16),
         pltpu.VMEM((CHUNKS, 32, EDGES), BF16),
-        pltpu.VMEM(chunked, BF16),
-        pltpu.VMEM(chunked, F32),
-        pltpu.VMEM(chunked, BF16),
-        pltpu.VMEM(chunked, BF16),
-        pltpu.VMEM(chunked, BF16),
+        pltpu.VMEM((CHUNKS, kinds, EDGES), BF16),
+        pltpu.VMEM(whole, F32),
+        pltpu.VMEM(whole, BF16),
+        pltpu.VMEM(whole, BF16),
+        pltpu.VMEM(whole, BF16),
+        pltpu.VMEM((9, 128, kinds), F32),
         pltpu.VMEM((9, 128, 128), F32),
         pltpu.VMEM((9, 128, 128), F32),
         pltpu.VMEM((9, 128, 128), F32),
@@ -490,7 +520,8 @@
         pltpu.VMEM((128, 128), BF16),
         pltpu.VMEM((2, 256, 128), BF16),
         pltpu.VMEM((2, 128, 256), BF16),
-        pltpu.VMEM((8, CHUNKS, EDGES), F32),
+        pltpu.VMEM(update_w.shape, BF16),
+        pltpu.SemaphoreType.DMA,
         pltpu.SemaphoreType.DMA((4, 8)),
         pltpu.SemaphoreType.DMA((4, 8)),
     ]
@@ -500,7 +531,7 @@
             jax.ShapeDtypeStruct((1, ATOMS), F32),
             jax.ShapeDtypeStruct((3, ATOMS), F32),
         ),
-        in_specs=[vmem] * 10,
+        in_specs=[vmem] * 8 + [pl.BlockSpec(memory_space=pl.ANY), vmem],
         out_specs=(vmem, vmem),
         scratch_shapes=scratch,
         compiler_params=pltpu.CompilerParams(
@@ -511,7 +542,7 @@
     )(
         positions,
         species.reshape(1, ATOMS),
-        neighbours,
+        neighbours.T,
         counts.reshape(1, ATOMS),
         send_x.reshape(2, 64),
         send_y.reshape(2, 128),

time: 77.7 us -> 56.9 us (0.73)
  Pallas kernels: 73 us -> 49.7 us
  local copies, waits for them, and re-layouts: 3.61 us -> 6.1 us
    pallas_call x1, Pallas kernels: 73 us -> 49.7 us  [body(): pl.pallas_call(functools.partial(kernel, remote), out_shape=(jax.ShapeDty...]
    unnamed x21 -> x22, local copies, waits for them, and re-layouts: 3.6 us -> 6.1 us
where the time goes in v2:
time: 56.9 us; the launch traced here: 56.4 us
  Pallas kernels  49.7 us (87%)
  local copies, waits for them, and re-layouts  6.1 us (11%)
  between operations  0.68 us (1%)
    pallas_call x1, Pallas kernels, body(): pl.pallas_call(functools.partial(kernel, remote), out_shape=(jax.ShapeDty...  49.7 us
    unnamed x22, local copies, waits for them, and re-layouts  6.1 us

profile of v2, /device:TPU:1, one launch (start us, length us, event | category | flops | bytes accessed | tf_op | source)
XLA Modules:
  0.0 56.4 jit_solution(1774018507855114339)
XLA Ops:
  0.6 0.0 copy-start.2
  0.6 0.0 copy-start.5
  0.7 0.0 copy-start.6
  0.7 0.0 copy-start.4
  0.7 0.7 %copy-done.2 = f32[2,8,128]{2,1,0:T(8,128)S(1)} copy-done((f32[2,8,128]{2,1,0:T(8,128)S(1)}, f32[2,8,128]{2,1,0:T(8,128)}, u32[]{:S(2)}) %copy-start.2) | copy-done | bytes 8216
  1.3 0.0 copy-done.5
  1.3 0.0 copy-done.6
  1.3 0.0 copy-done.4
  1.4 0.0 copy-start
  1.4 0.9 %copy-done = bf16[2,384,128]{2,1,0:T(8,128)(2,1)S(1)} copy-done((bf16[2,384,128]{2,1,0:T(8,128)(2,1)S(1)}, bf16[2,384,128]{2,1,0:T(8,128)(2,1)}, u32[]{:S(2)}) %copy-start) | copy-done | bytes 196632
  2.3 0.0 copy-start.1
  2.3 0.7 %copy-done.1 = s32[128,48]{0,1:T(8,128)S(1)} copy-done((s32[128,48]{0,1:T(8,128)S(1)}, s32[128,48]{0,1:T(8,128)}, u32[]{:S(2)}) %copy-start.1) | copy-done | bytes 24600
  3.0 0.0 copy-start.3
  3.0 0.7 %copy-done.3 = bf16[10,128]{1,0:T(8,128)(2,1)S(1)} copy-done((bf16[10,128]{1,0:T(8,128)(2,1)S(1)}, bf16[10,128]{1,0:T(8,128)(2,1)}, u32[]{:S(2)}) %copy-start.3) | copy-done | bytes 2584
  3.7 0.0 copy-start.7
  3.7 0.7 %copy-done.7 = s32[128]{0:T(128)S(1)} copy-done((s32[128]{0:T(128)S(1)}, s32[128]{0:T(128)}, u32[]{:S(2)}) %copy-start.7) | copy-done | bytes 536
  4.4 0.0 copy-start.8
  4.4 0.7 %copy-done.8 = s32[128]{0:T(128)S(1)} copy-done((s32[128]{0:T(128)S(1)}, s32[128]{0:T(128)}, u32[]{:S(2)}) %copy-start.8) | copy-done | bytes 536
  5.0 0.0 copy-start.9
  5.0 0.7 %copy-done.9 = f32[128]{0:T(128)S(1)} copy-done((f32[128]{0:T(128)S(1)}, f32[128]{0:T(128)}, u32[]{:S(2)}) %copy-start.9) | copy-done | bytes 536
  5.7 49.7 %shard_map.113 = (f32[1,128]{1,0:T(1,128)S(1)}, f32[3,128]{1,0:T(4,128)S(1)}) custom-call(bf16[3,128]{1,0:T(4,128)(2,1)S(1)} %copy-done.4, s32[1,128]{1,0:T(1,128)S(1)} %bitcast.10, s32[48,128]{1,0:T(8,128)S(1)} %bitcast.7, s32[1,128]{1,0:T(1,128)S(1)} %bitcast.11, s32[2,64]{1,0:T(2,128)S(1)} %bitcast.8, s32[2,128]{1,0:T(2,128)S(1)} %bitcast.9, ...), custom_call_target="tpu_custom_call" | custom-call | tf_op jit(solution)/shard_map/pallas_call | solution.py:528
  55.3 0.5 copy.14
  55.9 0.6 %copy.15 = f32[3,128]{1,0:T(4,128)} copy(f32[3,128]{1,0:T(4,128)S(1)} %get-tuple-element.9) | data formatting | bytes 3072
Async XLA Ops:
  0.6 0.7 %copy-start.2 = (f32[2,8,128]{2,1,0:T(8,128)S(1)}, f32[2,8,128]{2,1,0:T(8,128)}, u32[]{:S(2)}) copy-start(f32[2,8,128]{2,1,0:T(8,128)} %rw_ref.1) | copy-start | bytes 24580
  0.6 0.7 %copy-start.5 = (s32[1,2,64]{2,1,0:T(2,128)S(1)}, s32[1,2,64]{2,1,0:T(2,128)}, u32[]{:S(2)}) copy-start(s32[1,2,64]{2,1,0:T(2,128)} %param.14) | copy-start | bytes 1540
  0.7 0.7 %copy-start.6 = (s32[1,2,128]{2,1,0:T(2,128)S(1)}, s32[1,2,128]{2,1,0:T(2,128)}, u32[]{:S(2)}) copy-start(s32[1,2,128]{2,1,0:T(2,128)} %param.15) | copy-start | bytes 3076
  0.7 0.7 %copy-start.4 = (bf16[3,128]{1,0:T(4,128)(2,1)S(1)}, bf16[3,128]{1,0:T(4,128)(2,1)}, u32[]{:S(2)}) copy-start(bf16[3,128]{1,0:T(4,128)(2,1)} %pos_ref.1) | copy-start | bytes 2308
  1.4 0.9 %copy-start = (bf16[2,384,128]{2,1,0:T(8,128)(2,1)S(1)}, bf16[2,384,128]{2,1,0:T(8,128)(2,1)}, u32[]{:S(2)}) copy-start(bf16[2,384,128]{2,1,0:T(8,128)(2,1)} %uw_hbm.1) | copy-start | bytes 589828
  2.3 0.7 %copy-start.1 = (s32[128,48]{0,1:T(8,128)S(1)}, s32[128,48]{0,1:T(8,128)}, u32[]{:S(2)}) copy-start(s32[128,48]{0,1:T(8,128)} %param.12) | copy-start | bytes 73732
  3.0 0.7 %copy-start.3 = (bf16[10,128]{1,0:T(8,128)(2,1)S(1)}, bf16[10,128]{1,0:T(8,128)(2,1)}, u32[]{:S(2)}) copy-start(bf16[10,128]{1,0:T(8,128)(2,1)} %emb_ref.1) | copy-start | bytes 7684
  3.7 0.7 %copy-start.7 = (s32[128]{0:T(128)S(1)}, s32[128]{0:T(128)}, u32[]{:S(2)}) copy-start(s32[128]{0:T(128)} %param.11) | copy-start | bytes 1540
  4.4 0.7 %copy-start.8 = (s32[128]{0:T(128)S(1)}, s32[128]{0:T(128)}, u32[]{:S(2)}) copy-start(s32[128]{0:T(128)} %param.13) | copy-start | bytes 1540
  5.0 0.7 %copy-start.9 = (f32[128]{0:T(128)S(1)}, f32[128]{0:T(128)}, u32[]{:S(2)}) copy-start(f32[128]{0:T(128)} %param.19) | copy-start | bytes 1540

commit v3 on v2

--- a/solution.py
+++ b/solution.py
@@ -24,7 +24,7 @@
 NB = 8
 BOX = 8.0
 SCALE = 0.25
-SIDES = ((1, 0), (-1, 0), (0, 1), (0, -1), (1, 1), (1, -1), (-1, 1), (-1, -1))
+SIDES = ((0, 1), (0, -1), (1, 1), (1, -1), (-1, 1), (-1, -1), (1, 0), (-1, 0))
 R3, R5, R15 = math.sqrt(3.0), math.sqrt(5.0), math.sqrt(15.0)
 
 
@@ -56,16 +56,21 @@
 
 def kernel(
     remote,
-    pos_ref, spc_ref, nbr_ref, cnt_ref, sx_ref, sy_ref, emb_ref, rw_ref, uw_hbm, ow_ref,
-    en_ref, fo_ref,
-    geo_out, geo_x, geo_in, geo_xin,
+    *refs,
+):
+    inputs, out_ref, held, refs = refs[:10], refs[10], refs[11:21], refs[21:]
+    pos_ref, spc_ref, nbr_ref, cnt_ref, sx_ref, sy_ref, emb_ref, rw_ref, uw_ref, ow_ref = held
+    (geo_out, geo_x, geo_in, geo_xin,
     h_sec, h_own, h_piece,
     g_sec, g_own, g_piece,
     p_out, p_piece, p_own, p_pin,
-    nbr_t, nbr_d, spc_d, vec_d, harm_t, hot, hmat, hlow, basis, phi, rad2, gat2, gms, rows_t,
+    nbr_t, nbr_d, spc_d, vec_d, harm_t, hot, hmat, basis, phi, rad2, gat2, gms, rows_t,
     kinds_amps, amps1, amps2, gamps, z1_ref, gext, gharm, ohx, ohxt, ohy, ohyt,
-    uw_ref, uw_sem, send_sem, recv_sem,
-):
+    in_sem, send_sem, recv_sem) = refs
+    loads = [
+        pltpu.make_async_copy(src, dst, in_sem.at[number])
+        for number, (src, dst) in enumerate(zip(inputs, held))
+    ]
     if remote:
         nx, ny = lax.axis_size("gx"), lax.axis_size("gy")
         me_x, me_y = lax.axis_index("gx"), lax.axis_index("gy")
@@ -77,9 +82,11 @@
         for side in SIDES:
             pl.semaphore_signal(barrier, inc=1, device_id=place(side), device_id_type=MESH)
 
-    def exchange(phase, parts):
+    def exchange(phase, parts, only=None):
         copies = []
         for number, side in enumerate(SIDES):
+            if only is not None and not only(side):
+                continue
             src, dst = parts(side)
             if remote:
                 copy = pltpu.make_async_remote_copy(
@@ -97,8 +104,10 @@
         for copy in copies:
             copy.wait()
 
-    weights = pltpu.make_async_copy(uw_hbm, uw_ref, uw_sem)
-    weights.start()
+    for number in (0, 1, 4, 5, 2, 3, 6, 7, 9, 8):
+        loads[number].start()
+    for number in (0, 1, 4, 5):
+        loads[number].wait()
 
     sx = jnp.concatenate([sx_ref[0:1, :], sx_ref[1:2, :]], axis=1)
     sel = jnp.where(iota((ATOMS, 128), 0) == sx, 1.0, 0.0)
@@ -125,6 +134,7 @@
 
     copies = exchange(0, geo_parts)
 
+    loads[2].wait()
     nbr_t[...] = nbr_ref[...].T
     nbr_d[...] = jnp.concatenate(
         [nbr_t[pl.ds(a, CHUNKS, stride=GROUP), :] for a in range(GROUP)], axis=1
@@ -153,6 +163,8 @@
     atom = iota((CHUNKS, EDGES), 0) * GROUP + of_lane
     mask = of_lane[:GROUP] == iota((GROUP, EDGES), 0)
 
+    for number in (3, 6, 7, 9):
+        loads[number].wait()
     high, low = split(rw_ref[1])
     w_t = jnp.concatenate([high, high, low, jnp.zeros_like(high)], axis=0).T.astype(BF16)
     w_rows = jnp.concatenate([high, low], axis=0).astype(BF16)
@@ -234,8 +246,11 @@
         return away, jnp.exp(-0.125 * away * away) * vec_d[1, pl.ds(g, 1), :]
 
     def sums_of(g, high, low):
-        left = jnp.concatenate([hmat[g], hlow[g], hmat[g]], axis=1)
-        return nt(left, jnp.concatenate([high, high, low], axis=1))
+        fill = jnp.zeros((128 - high.shape[0], EDGES), BF16)
+        right = [high, low] if high.shape[0] == 128 else [high, fill, low]
+        both = nt(hmat[g], jnp.concatenate(right, axis=0))
+        n = high.shape[0]
+        return both[:80, :n] + both[:80, 128 : 128 + n] + both[80:, :n]
 
     def store_sums(ref, g, sums):
         at = pl.ds(pl.multiple_of(g * GROUP, GROUP), GROUP)
@@ -249,8 +264,8 @@
             rows.append(jnp.where(mask, harm_t[m, pl.ds(g, 1), :], 0.0))
         rows.append(jnp.zeros((GROUP, EDGES), F32))
         rows, fine = split(jnp.concatenate(rows, axis=0))
-        hmat[g] = rows.astype(BF16)
-        hlow[g] = fine.astype(BF16)
+        hmat[g, 0:80] = rows.astype(BF16)
+        hmat[g, 80:160] = fine.astype(BF16)
         high, low = split(radial_basis(g)[1])
         basis[g] = jnp.concatenate([high, low, high, jnp.zeros_like(high)], axis=0).astype(BF16)
         kind = spc_d[pl.ds(g, 1), :]
@@ -266,7 +281,7 @@
     for m in range(9):
         high, low = (v.astype(BF16) for v in split(kinds_amps[m]))
         amps1[m] = mm(high, kind_high) + mm(low, kind_high) + mm(high, kind_low)
-    weights.wait()
+    loads[8].wait()
 
     def update(amps, old, t):
         one = amps[1] * amps[1] + amps[2] * amps[2] + amps[3] * amps[3]
@@ -293,7 +308,6 @@
     z1_ref[...] = z1
     h_sec[1, 0:128] = h1
     h_own[...] = h1
-    h_piece[...] = mm(ohxt[...], h1).astype(BF16)
 
     def h_parts(side):
         dx, dy = side
@@ -303,7 +317,9 @@
             return h_piece.at[pl.ds(0, 64)], h_sec.at[1 - dy, pl.ds(128, 64)]
         return h_piece.at[pl.ds(64, 64)], h_sec.at[1 - dy, pl.ds(192, 64)]
 
-    copies = exchange(1, h_parts)
+    copies = exchange(1, h_parts, lambda side: side[0] == 0)
+    h_piece[...] = mm(ohxt[...], h1).astype(BF16)
+    copies += exchange(1, h_parts, lambda side: side[0] != 0)
 
     def second_radial(g, carry):
         rad2[:, lanes(g)] = mm(w_t, basis[g])
@@ -328,14 +344,9 @@
             store_sums(amps2, g, sums_of(g, high, low))
         return carry
 
-    lax.fori_loop(0, PAIRS, second, 0, unroll=4)
+    lax.fori_loop(0, PAIRS, second, 0, unroll=8)
     z2, h2 = update(amps2, h1.astype(F32), 1)
     out_w = ow_ref[...]
-    high, rest = split(out_w)
-    mid, low = split(rest)
-    readout = jnp.concatenate([high, mid, low, jnp.zeros((5, 128), F32)], axis=0).astype(BF16)
-    parts = nt(readout, h2)
-    en_ref[...] = parts[0:1] + parts[1:2] + parts[2:3]
     back(amps2, z2, out_w, 1)
 
     def chunk_rows(ref, g):
@@ -344,17 +355,15 @@
         return jnp.concatenate(rows + [jnp.zeros_like(rows[0])], axis=0)
 
     def features(g, carry):
-        grad = mm(chunk_rows(gamps, g).T.astype(BF16), hmat[g])
+        grad = mm(chunk_rows(gamps, g).T.astype(BF16), hmat[g, 0:80])
         gms[:, lanes(g)] = grad.astype(BF16)
         rows_t[:, lanes(g)] = (grad * rad2[:, lanes(g)]).astype(BF16)
         return carry
 
     lax.fori_loop(0, CHUNKS, features, 0, unroll=8)
-    gext[...] = nt(hot[...], rows_t[...])
-
-    for number, start in ((0, 256), (1, 384)):
-        g_sec[2 * number] = mm(ohy[number], gext[start : start + 128].astype(BF16)).astype(BF16)
-    g_sec[1, 128:256] = gext[128:256].astype(BF16)
+    far_rows = nt(hot[256:512], rows_t[...]).astype(BF16)
+    for number in range(2):
+        g_sec[2 * number] = mm(ohy[number], far_rows[128 * number : 128 * number + 128]).astype(BF16)
 
     def g_parts(side):
         dx, dy = side
@@ -364,7 +373,17 @@
             return g_sec.at[1 + dy, pl.ds(128, 64)], g_piece.at[1 - dy, pl.ds(0, 64)]
         return g_sec.at[1 + dy, pl.ds(192, 64)], g_piece.at[1 - dy, pl.ds(64, 64)]
 
-    copies = exchange(2, g_parts)
+    copies = exchange(2, g_parts, lambda side: side[1] != 0)
+    near_rows = nt(hot[0:256], rows_t[...])
+    g_sec[1, 128:256] = near_rows[128:256].astype(BF16)
+    copies += exchange(2, g_parts, lambda side: side[1] == 0)
+    gext[...] = near_rows[0:128]
+
+    high, rest = split(out_w)
+    mid, low = split(rest)
+    readout = jnp.concatenate([high, mid, low, jnp.zeros((5, 128), F32)], axis=0).astype(BF16)
+    parts = nt(readout, h2)
+    energy = parts[0:1] + parts[1:2] + parts[2:3]
 
     def harmonic_rows(wide):
         rows = []
@@ -390,7 +409,7 @@
     lax.fori_loop(0, CHUNKS, geometry_two, 0, unroll=8)
     finish(copies)
 
-    grad_h1 = gext[0:128] + out_w + g_own[0].astype(F32) + g_own[1].astype(F32)
+    grad_h1 = gext[...] + out_w + g_own[0].astype(F32) + g_own[1].astype(F32)
     piece = g_piece[0].astype(F32) + g_piece[1].astype(F32) + g_piece[2].astype(F32)
     grad_h1 += mm(ohx[...], piece.astype(BF16))
     back(amps1, z1_ref[...], grad_h1, 0)
@@ -401,7 +420,7 @@
     def geometry_one(g, carry):
         grads = chunk_rows(kinds_amps, g)
         rows = harmonic_rows(mm(grads.astype(BF16), phi[g]))
-        by_kind = mm(grads.T.astype(BF16), hmat[g])
+        by_kind = mm(grads.T.astype(BF16), hmat[g, 0:80])
         kind = spc_d[pl.ds(g, 1), :]
         by_basis = jnp.where(kind == 0, by_kind[0:NB], 0.0)
         for k in range(1, species):
@@ -473,11 +492,15 @@
     piece = jnp.where(iota((8, 128), 1) < 64, up, down)[0:3]
     result = total[:, 0:128] - own_rows + p_own[0][0:3] + p_own[1][0:3]
     result += three(nt(six(piece), ohx[...]))
-    fo_ref[...] = -result
+    out_ref[...] = jnp.concatenate([energy, -result, jnp.zeros((4, 128), F32)], axis=0)
+
+
+def divide(out_ref, energy_ref, forces_ref):
+    energy_ref[...] = out_ref[0:1]
+    forces_ref[...] = out_ref[1:4]
 
 
 def body(remote, positions, species, neighbours, counts, send_x, send_y, embed, radial_w, update_w, out_w):
-    vmem = pl.BlockSpec(memory_space=pltpu.VMEM)
     kinds = embed.shape[0] * NB
     whole = (128, CHUNKS * EDGES)
     scratch = [
@@ -501,8 +524,7 @@
         pltpu.VMEM((6, CHUNKS, EDGES), F32),
         pltpu.VMEM((8, CHUNKS, EDGES), F32),
         pltpu.VMEM((EXT, CHUNKS * EDGES), BF16),
-        pltpu.VMEM((CHUNKS, 80, EDGES), BF16),
-        pltpu.VMEM((CHUNKS, 80, EDGES), BF16),
+        pltpu.VMEM((CHUNKS, 160, EDGES), BF16),
         pltpu.VMEM((CHUNKS, 32, EDGES), BF16),
         pltpu.VMEM((CHUNKS, kinds, EDGES), BF16),
         pltpu.VMEM(whole, F32),
@@ -514,32 +536,17 @@
         pltpu.VMEM((9, 128, 128), F32),
         pltpu.VMEM((9, 128, 128), F32),
         pltpu.VMEM((128, 128), F32),
-        pltpu.VMEM((EXT, 128), F32),
+        pltpu.VMEM((128, 128), F32),
         pltpu.VMEM((9, CHUNKS, EDGES), F32),
         pltpu.VMEM((128, 128), BF16),
         pltpu.VMEM((128, 128), BF16),
         pltpu.VMEM((2, 256, 128), BF16),
         pltpu.VMEM((2, 128, 256), BF16),
-        pltpu.VMEM(update_w.shape, BF16),
-        pltpu.SemaphoreType.DMA,
+        pltpu.SemaphoreType.DMA((10,)),
         pltpu.SemaphoreType.DMA((4, 8)),
         pltpu.SemaphoreType.DMA((4, 8)),
     ]
-    energy, forces = pl.pallas_call(
-        functools.partial(kernel, remote),
-        out_shape=(
-            jax.ShapeDtypeStruct((1, ATOMS), F32),
-            jax.ShapeDtypeStruct((3, ATOMS), F32),
-        ),
-        in_specs=[vmem] * 8 + [pl.BlockSpec(memory_space=pl.ANY), vmem],
-        out_specs=(vmem, vmem),
-        scratch_shapes=scratch,
-        compiler_params=pltpu.CompilerParams(
-            collective_id=0 if remote else None,
-            has_side_effects=remote,
-            vmem_limit_bytes=48 * 1024 * 1024,
-        ),
-    )(
+    inputs = (
         positions,
         species.reshape(1, ATOMS),
         neighbours.T,
@@ -551,6 +558,25 @@
         update_w,
         out_w.reshape(1, WIDTH),
     )
+    out = pl.pallas_call(
+        functools.partial(kernel, remote),
+        out_shape=jax.ShapeDtypeStruct((8, ATOMS), F32),
+        in_specs=[pl.BlockSpec(memory_space=pl.ANY)] * len(inputs),
+        out_specs=pl.BlockSpec(memory_space=pltpu.VMEM),
+        scratch_shapes=[pltpu.VMEM(v.shape, v.dtype) for v in inputs] + scratch,
+        compiler_params=pltpu.CompilerParams(
+            collective_id=0 if remote else None,
+            has_side_effects=remote,
+            vmem_limit_bytes=60 * 1024 * 1024,
+        ),
+    )(*inputs)
+    energy, forces = pl.pallas_call(
+        divide,
+        out_shape=(
+            jax.ShapeDtypeStruct((1, ATOMS), F32),
+            jax.ShapeDtypeStruct((3, ATOMS), F32),
+        ),
+    )(out)
     return energy.reshape(ATOMS), forces
 
 

time: 56.9 us -> 50.9 us (0.89)
  local copies, waits for them, and re-layouts: 6.1 us -> 0 us
    unnamed x22 -> x0, local copies, waits for them, and re-layouts: 6.1 us -> none
    pallas_call x1 -> x2, Pallas kernels: 49.7 us -> 50.1 us  [the longest x1 48.8 us: body(): pl.pallas_call(functools.partial(kernel, remote), out_shape=jax.ShapeDtyp...]
where the time goes in v3:
time: 50.9 us; the launch traced here: 50.7 us
  Pallas kernels  50.1 us (98%)
  between operations  0.64 us (1%)
    pallas_call x1, Pallas kernels, body(): pl.pallas_call(functools.partial(kernel, remote), out_shape=jax.ShapeDtyp...  48.8 us
    pallas_call x1, Pallas kernels, body(): pl.pallas_call(divide, out_shape=(jax.ShapeDtypeStruct((1, ATOMS), F32),...  1.26 us

profile of v3, /device:TPU:1, one launch (start us, length us, event | category | flops | bytes accessed | tf_op | source)
XLA Modules:
  0.0 50.7 jit_solution(14654948849149024700)
XLA Ops:
  0.6 48.8 %shard_map.113.out_ref = f32[8,128]{1,0:T(8,128)} custom-call(bf16[3,128]{1,0:T(4,128)(2,1)} %refs_0_.1, s32[1,128]{1,0:T(1,128)} %bitcast.10, s32[48,128]{1,0:T(8,128)} %bitcast.7, s32[1,128]{1,0:T(1,128)} %bitcast.11, s32[2,64]{1,0:T(2,128)} %bitcast.8, s32[2,128]{1,0:T(2,128)} %bitcast.9, bf16[10,128]{1,0:T(8,128)(2,1)} %refs_6_.1, f32[2,8,128]{2,1,0:T(8,128)} %refs_7_.1, ...), custom_call_target="tpu_custom_call" | custom-call | tf_op jit(solution)/shard_map/pallas_call | solution.py:561
  49.5 1.3 %shard_map.114 = (f32[1,128]{1,0:T(1,128)}, f32[3,128]{1,0:T(4,128)}) custom-call(f32[8,128]{1,0:T(8,128)} %shard_map.113.out_ref), custom_call_target="tpu_custom_call" | custom-call | tf_op jit(solution)/shard_map/pallas_call | solution.py:573

commit v4 on v3

--- a/solution.py
+++ b/solution.py
@@ -58,14 +58,14 @@
     remote,
     *refs,
 ):
-    inputs, out_ref, held, refs = refs[:10], refs[10], refs[11:21], refs[21:]
+    inputs, en_ref, fo_ref, held, refs = refs[:10], refs[10], refs[11], refs[12:22], refs[22:]
     pos_ref, spc_ref, nbr_ref, cnt_ref, sx_ref, sy_ref, emb_ref, rw_ref, uw_ref, ow_ref = held
     (geo_out, geo_x, geo_in, geo_xin,
     h_sec, h_own, h_piece,
     g_sec, g_own, g_piece,
     p_out, p_piece, p_own, p_pin,
-    nbr_t, nbr_d, spc_d, vec_d, harm_t, hot, hmat, basis, phi, rad2, gat2, gms, rows_t,
-    kinds_amps, amps1, amps2, gamps, z1_ref, gext, gharm, ohx, ohxt, ohy, ohyt,
+    nbr_t, nbr_d, spc_d, vec_d, harm_t, hot, low_hot, hmat, basis, phi, rad2, gat2, gms, rows_t,
+    kinds_amps, amps1, amps2, gamps, z1_ref, gext, gharm, gdist, ohx, ohxt, ohy, ohyt,
     in_sem, send_sem, recv_sem) = refs
     loads = [
         pltpu.make_async_copy(src, dst, in_sem.at[number])
@@ -151,6 +151,11 @@
             hot[16 * block : 16 * block + 16, lanes(g)] = jnp.where(
                 index - jnp.int16(16 * block) == first_rows, one, none
             )
+        lower = index & jnp.int16(63)
+        for block in range(4):
+            low_hot[16 * block : 16 * block + 16, lanes(g)] = jnp.where(
+                lower - jnp.int16(16 * block) == first_rows, one, none
+            )
         return carry
 
     lax.fori_loop(0, CHUNKS, build, 0, unroll=8)
@@ -238,7 +243,7 @@
         0.5 * R5 * (3.0 * uz * uz - 1.0), R15 * ux * uz, 0.5 * R15 * (ux * ux - uy * uy),
     )
     for number, value in enumerate(harm):
-        harm_t[number] = SCALE * value
+        harm_t[number], harm_t[8 + number] = split(SCALE * value)
 
     def radial_basis(g):
         centers = 1.0 + 2.0 * iota((NB, EDGES), 0).astype(F32)
@@ -258,23 +263,27 @@
             ref[m, at, :] = sums[m * GROUP : (m + 1) * GROUP]
 
     def first(g, carry):
-        unit = jnp.where(mask, SCALE, 0.0)
-        rows = [unit]
+        none = jnp.zeros((GROUP, EDGES), F32)
+        rows = [jnp.where(mask, SCALE, 0.0)]
+        fine = [none]
         for m in range(8):
             rows.append(jnp.where(mask, harm_t[m, pl.ds(g, 1), :], 0.0))
-        rows.append(jnp.zeros((GROUP, EDGES), F32))
-        rows, fine = split(jnp.concatenate(rows, axis=0))
-        hmat[g, 0:80] = rows.astype(BF16)
-        hmat[g, 80:160] = fine.astype(BF16)
+            fine.append(jnp.where(mask, harm_t[8 + m, pl.ds(g, 1), :], 0.0))
+        hmat[g, 0:80] = jnp.concatenate(rows + [none], axis=0).astype(BF16)
+        hmat[g, 80:160] = jnp.concatenate(fine + [none], axis=0).astype(BF16)
         high, low = split(radial_basis(g)[1])
-        basis[g] = jnp.concatenate([high, low, high, jnp.zeros_like(high)], axis=0).astype(BF16)
-        kind = spc_d[pl.ds(g, 1), :]
-        phi_high, phi_low = (
-            jnp.concatenate([jnp.where(kind == k, v, 0.0) for k in range(species)], axis=0)
-            for v in (high, low)
-        )
-        phi[g] = phi_high.astype(BF16)
-        store_sums(kinds_amps, g, sums_of(g, phi[g], phi_low.astype(BF16)))
+        basis[g] = jnp.concatenate([high, low, high, none], axis=0).astype(BF16)
+        kind = jnp.broadcast_to(spc_d[pl.ds(g, 1), :], (16, EDGES)).astype(jnp.int16)
+        kind -= (iota((16, EDGES), 0) >= 8).astype(jnp.int16)
+        high, low = (jnp.concatenate([v, v], axis=0).astype(BF16) for v in (high, low))
+        none = jnp.zeros((16, EDGES), BF16)
+        phi_low = []
+        for pair in range(species // 2):
+            here = kind == jnp.int16(2 * pair)
+            phi[g, 16 * pair : 16 * pair + 16] = jnp.where(here, high, none)
+            phi_low.append(jnp.where(here, low, none))
+        phi_low = jnp.concatenate(phi_low, axis=0)
+        store_sums(kinds_amps, g, sums_of(g, phi[g], phi_low))
         return carry
 
     lax.fori_loop(0, CHUNKS, first, 0, unroll=8)
@@ -334,17 +343,23 @@
     high_t = mm(ohyt[1], h_sec[2]).T
     h_t = jnp.concatenate([own_t, got_t, low_t, high_t], axis=1).astype(BF16)
 
-    def second(p, carry):
+    def gather(p):
         gathered = mm(h_t, hot[:, lanes(p, 2)])
         gat2[:, lanes(p, 2)] = gathered.astype(BF16)
+
+    def second(p, last):
+        if not last:
+            gather(p + 1)
         for half in range(2):
             g = 2 * p + half
-            message = gathered[:, half * EDGES : (half + 1) * EDGES] * rad2[:, lanes(g)]
-            high, low = (v.astype(BF16) for v in split(message))
+            high, low = (
+                v.astype(BF16) for v in split(gat2[:, lanes(g)].astype(F32) * rad2[:, lanes(g)])
+            )
             store_sums(amps2, g, sums_of(g, high, low))
-        return carry
-
-    lax.fori_loop(0, PAIRS, second, 0, unroll=8)
+
+    gather(0)
+    for p in range(PAIRS):
+        second(p, p == PAIRS - 1)
     z2, h2 = update(amps2, h1.astype(F32), 1)
     out_w = ow_ref[...]
     back(amps2, z2, out_w, 1)
@@ -354,14 +369,19 @@
         rows = [ref[m, at, :] for m in range(9)]
         return jnp.concatenate(rows + [jnp.zeros_like(rows[0])], axis=0)
 
-    def features(g, carry):
-        grad = mm(chunk_rows(gamps, g).T.astype(BF16), hmat[g, 0:80])
-        gms[:, lanes(g)] = grad.astype(BF16)
-        rows_t[:, lanes(g)] = (grad * rad2[:, lanes(g)]).astype(BF16)
-        return carry
-
-    lax.fori_loop(0, CHUNKS, features, 0, unroll=8)
-    far_rows = nt(hot[256:512], rows_t[...]).astype(BF16)
+    def features(p):
+        for g in (2 * p, 2 * p + 1):
+            grad = mm(chunk_rows(gamps, g).T.astype(BF16), hmat[g, 0:80])
+            gms[:, lanes(g)] = grad.astype(BF16)
+            rows_t[:, lanes(g)] = (grad * rad2[:, lanes(g)]).astype(BF16)
+
+    features(0)
+    far_rows = jnp.zeros((256, 128), F32)
+    for p in range(PAIRS):
+        if p + 1 < PAIRS:
+            features(p + 1)
+        far_rows += nt(hot[256:512, lanes(p, 2)], rows_t[:, lanes(p, 2)])
+    far_rows = far_rows.astype(BF16)
     for number in range(2):
         g_sec[2 * number] = mm(ohy[number], far_rows[128 * number : 128 * number + 128]).astype(BF16)
 
@@ -383,14 +403,22 @@
     mid, low = split(rest)
     readout = jnp.concatenate([high, mid, low, jnp.zeros((5, 128), F32)], axis=0).astype(BF16)
     parts = nt(readout, h2)
-    energy = parts[0:1] + parts[1:2] + parts[2:3]
+    en_ref[...] = parts[0:1] + parts[1:2] + parts[2:3]
 
     def harmonic_rows(wide):
-        rows = []
-        for m in range(1, 9):
-            part = jnp.where(mask, wide[m * GROUP : (m + 1) * GROUP], 0.0)
-            rows.append(jnp.sum(part, axis=0, keepdims=True))
-        return rows
+        which = of_lane[:GROUP]
+        result = jnp.zeros((8, EDGES), F32)
+        for m in range(8):
+            part = wide[(m + 1) * GROUP : (m + 2) * GROUP]
+            part = jnp.concatenate(
+                [
+                    jnp.take_along_axis(part[:, t : t + 128], which[:, t : t + 128], axis=0)
+                    for t in range(0, EDGES, 128)
+                ],
+                axis=1,
+            )
+            result = jnp.where(iota((8, EDGES), 0) == m, part, result)
+        return result
 
     def distance_row(g, by_basis):
         away, value = radial_basis(g)
@@ -399,11 +427,9 @@
     def geometry_two(g, carry):
         gathered = gat2[:, lanes(g)].astype(F32)
         message = (gathered * rad2[:, lanes(g)]).astype(BF16)
-        rows = harmonic_rows(mm(chunk_rows(gamps, g).astype(BF16), message))
+        gharm[g] = harmonic_rows(mm(chunk_rows(gamps, g).astype(BF16), message))
         two = mm(w_rows, (gms[:, lanes(g)].astype(F32) * gathered).astype(BF16))
-        rows.append(distance_row(g, two[0:NB] + two[NB:]))
-        for number, value in enumerate(rows):
-            gharm[number, pl.ds(g, 1), :] = value
+        gdist[pl.ds(g, 1), :] = distance_row(g, two[0:NB] + two[NB:])
         return carry
 
     lax.fori_loop(0, CHUNKS, geometry_two, 0, unroll=8)
@@ -419,25 +445,23 @@
 
     def geometry_one(g, carry):
         grads = chunk_rows(kinds_amps, g)
-        rows = harmonic_rows(mm(grads.astype(BF16), phi[g]))
+        gharm[g] += harmonic_rows(mm(grads.astype(BF16), phi[g]))
         by_kind = mm(grads.T.astype(BF16), hmat[g, 0:80])
-        kind = spc_d[pl.ds(g, 1), :]
+        kind = jnp.broadcast_to(spc_d[pl.ds(g, 1), :], (NB, EDGES))
         by_basis = jnp.where(kind == 0, by_kind[0:NB], 0.0)
         for k in range(1, species):
             by_basis += jnp.where(kind == k, by_kind[k * NB : (k + 1) * NB], 0.0)
-        rows.append(distance_row(g, by_basis))
-        for number, value in enumerate(rows):
-            gharm[number, pl.ds(g, 1), :] += value
+        gdist[pl.ds(g, 1), :] += distance_row(g, by_basis)
         return carry
 
     lax.fori_loop(0, CHUNKS, geometry_one, 0, unroll=8)
 
     inv, vx, vy, vz = (vec_d[n] for n in range(2, 6))
-    g1, g2, g3, g4, g5, g6, g7, g8 = (SCALE * gharm[n] for n in range(8))
+    g1, g2, g3, g4, g5, g6, g7, g8 = (SCALE * gharm[:, n, :] for n in range(8))
     gx = R3 * g1 + R15 * (vy * g4 + vz * g7 + vx * g8)
     gy = R3 * g2 + R15 * (vx * g4 + vz * g5 - vy * g8)
     gz = R3 * g3 + R15 * (vy * g5 + vx * g7) + 3.0 * R5 * vz * g6
-    along = gharm[8] - inv * (gx * vx + gy * vy + gz * vz)
+    along = gdist[...] - inv * (gx * vx + gy * vy + gz * vz)
     wide_rows = []
     for grad, unit in ((gx, vx), (gy, vy), (gz, vz)):
         wide_rows += split(grad * inv + unit * along)
@@ -450,15 +474,14 @@
         both = sums[32 * number : 32 * number + 16] + sums[32 * number + 16 : 32 * number + 32]
         own_rows.append(jnp.sum(jnp.where(here, both, 0.0), axis=0, keepdims=True))
 
-    upper, lower = nbr >> 6, nbr & 63
-    left, right = [], []
+    upper = nbr >> 6
+    left = []
     for g in range(CHUNKS):
         here = iota((8, EDGES), 0) == upper[g : g + 1]
         left.append(
             jnp.concatenate([jnp.where(here, v[g : g + 1], 0.0) for v in wide_rows], axis=0).astype(BF16)
         )
-        right.append(onehot(lower[g : g + 1], 64))
-    both = nt(jnp.concatenate(left, axis=1), jnp.concatenate(right, axis=1))
+    both = nt(jnp.concatenate(left, axis=1), low_hot[...])
     coords = []
     for number in range(3):
         value = both[16 * number : 16 * number + 8] + both[16 * number + 8 : 16 * number + 16]
@@ -492,12 +515,18 @@
     piece = jnp.where(iota((8, 128), 1) < 64, up, down)[0:3]
     result = total[:, 0:128] - own_rows + p_own[0][0:3] + p_own[1][0:3]
     result += three(nt(six(piece), ohx[...]))
-    out_ref[...] = jnp.concatenate([energy, -result, jnp.zeros((4, 128), F32)], axis=0)
-
-
-def divide(out_ref, energy_ref, forces_ref):
-    energy_ref[...] = out_ref[0:1]
-    forces_ref[...] = out_ref[1:4]
+    fo_ref[...] = -result
+
+
+def place_outputs(energy_in, forces_in, energy_ref, forces_ref, sems):
+    copies = [
+        pltpu.make_async_copy(energy_in, energy_ref, sems.at[0]),
+        pltpu.make_async_copy(forces_in, forces_ref, sems.at[1]),
+    ]
+    for copy in copies:
+        copy.start()
+    for copy in copies:
+        copy.wait()
 
 
 def body(remote, positions, species, neighbours, counts, send_x, send_y, embed, radial_w, update_w, out_w):
@@ -522,8 +551,9 @@
         pltpu.VMEM((CHUNKS, EDGES), I32),
         pltpu.VMEM((CHUNKS, EDGES), I32),
         pltpu.VMEM((6, CHUNKS, EDGES), F32),
-        pltpu.VMEM((8, CHUNKS, EDGES), F32),
+        pltpu.VMEM((16, CHUNKS, EDGES), F32),
         pltpu.VMEM((EXT, CHUNKS * EDGES), BF16),
+        pltpu.VMEM((64, CHUNKS * EDGES), BF16),
         pltpu.VMEM((CHUNKS, 160, EDGES), BF16),
         pltpu.VMEM((CHUNKS, 32, EDGES), BF16),
         pltpu.VMEM((CHUNKS, kinds, EDGES), BF16),
@@ -537,7 +567,8 @@
         pltpu.VMEM((9, 128, 128), F32),
         pltpu.VMEM((128, 128), F32),
         pltpu.VMEM((128, 128), F32),
-        pltpu.VMEM((9, CHUNKS, EDGES), F32),
+        pltpu.VMEM((CHUNKS, 8, EDGES), F32),
+        pltpu.VMEM((CHUNKS, EDGES), F32),
         pltpu.VMEM((128, 128), BF16),
         pltpu.VMEM((128, 128), BF16),
         pltpu.VMEM((2, 256, 128), BF16),
@@ -558,11 +589,15 @@
         update_w,
         out_w.reshape(1, WIDTH),
     )
-    out = pl.pallas_call(
+    shapes = (
+        jax.ShapeDtypeStruct((1, ATOMS), F32),
+        jax.ShapeDtypeStruct((3, ATOMS), F32),
+    )
+    results = pl.pallas_call(
         functools.partial(kernel, remote),
-        out_shape=jax.ShapeDtypeStruct((8, ATOMS), F32),
+        out_shape=shapes,
         in_specs=[pl.BlockSpec(memory_space=pl.ANY)] * len(inputs),
-        out_specs=pl.BlockSpec(memory_space=pltpu.VMEM),
+        out_specs=(pl.BlockSpec(memory_space=pltpu.VMEM), pl.BlockSpec(memory_space=pltpu.VMEM)),
         scratch_shapes=[pltpu.VMEM(v.shape, v.dtype) for v in inputs] + scratch,
         compiler_params=pltpu.CompilerParams(
             collective_id=0 if remote else None,
@@ -570,13 +605,15 @@
             vmem_limit_bytes=60 * 1024 * 1024,
         ),
     )(*inputs)
+    anywhere = pl.BlockSpec(memory_space=pl.ANY)
     energy, forces = pl.pallas_call(
-        divide,
-        out_shape=(
-            jax.ShapeDtypeStruct((1, ATOMS), F32),
-            jax.ShapeDtypeStruct((3, ATOMS), F32),
-        ),
-    )(out)
+        place_outputs,
+        out_shape=shapes,
+        in_specs=[anywhere, anywhere],
+        out_specs=(anywhere, anywhere),
+        scratch_shapes=[pltpu.SemaphoreType.DMA((2,))],
+        compiler_params=pltpu.CompilerParams(vmem_limit_bytes=60 * 1024 * 1024),
+    )(*results)
     return energy.reshape(ATOMS), forces
 
 

time: 50.9 us -> 49.3 us (0.969)
  Pallas kernels: 50.1 us -> 48.6 us
    pallas_call x2, Pallas kernels: 50.1 us -> 48.6 us  [the longest x1 47.4 us: body(): pl.pallas_call(functools.partial(kernel, remote), out_shape=shapes, in_sp...]
where the time goes in v4:
time: 49.3 us; the launch traced here: 49.2 us
  Pallas kernels  48.6 us (99%)
  between operations  0.64 us (1%)
    pallas_call x1, Pallas kernels, body(): pl.pallas_call(functools.partial(kernel, remote), out_shape=shapes, in_sp...  47.4 us
    pallas_call x1, Pallas kernels, body(): pl.pallas_call(place_outputs, out_shape=shapes, in_specs=[anywhere, anywh...  1.18 us

profile of v4, /device:TPU:1, one launch (start us, length us, event | category | flops | bytes accessed | tf_op | source)
XLA Modules:
  0.0 49.2 jit_solution(5022006081750308913)
XLA Ops:
  0.6 47.4 %shard_map.113 = (f32[1,128]{1,0:T(1,128)}, f32[3,128]{1,0:T(4,128)}) custom-call(bf16[3,128]{1,0:T(4,128)(2,1)} %refs_0_.1, s32[1,128]{1,0:T(1,128)} %bitcast.10, s32[48,128]{1,0:T(8,128)} %bitcast.7, s32[1,128]{1,0:T(1,128)} %bitcast.11, s32[2,64]{1,0:T(2,128)} %bitcast.8, s32[2,128]{1,0:T(2,128)} %bitcast.9, bf16[10,128]{1,0:T(8,128)(2,1)} %refs_6_.1, ...), custom_call_target="tpu_custom_call" | custom-call | tf_op jit(solution)/shard_map/pallas_call | solution.py:596
  48.1 1.2 %shard_map.114 = (f32[1,128]{1,0:T(1,128)}, f32[3,128]{1,0:T(4,128)}) custom-call(f32[1,128]{1,0:T(1,128)} %get-tuple-element.6.energy_in, f32[3,128]{1,0:T(4,128)} %get-tuple-element.7.forces_in), custom_call_target="tpu_custom_call" | custom-call | tf_op jit(solution)/shard_map/pallas_call | solution.py:609

commit v5 on v4

--- a/solution.py
+++ b/solution.py
@@ -75,8 +75,11 @@
         nx, ny = lax.axis_size("gx"), lax.axis_size("gy")
         me_x, me_y = lax.axis_index("gx"), lax.axis_index("gy")
 
+        xs = (me_x, lax.rem(me_x + 1, nx), lax.rem(me_x + nx - 1, nx))
+        ys = (me_y, lax.rem(me_y + 1, ny), lax.rem(me_y + ny - 1, ny))
+
         def place(side):
-            return (lax.rem(me_x + side[0] + nx, nx), lax.rem(me_y + side[1] + ny, ny))
+            return (xs[side[0]], ys[side[1]])
 
         barrier = pltpu.get_barrier_semaphore()
         for side in SIDES:
@@ -300,9 +303,12 @@
         z = mm(flat, uw_ref[t])
         return z, (old + z * jax.nn.sigmoid(z)).astype(BF16)
 
-    def back(amps, z, grad, t):
+    def slope(z):
         sig = jax.nn.sigmoid(z)
-        grad_z = grad * (sig * (1.0 + z * (1.0 - sig)))
+        return sig * (1.0 + z * (1.0 - sig))
+
+    def back(amps, steep, grad, t):
+        grad_z = grad * steep
         grad_inv = nt(grad_z.astype(BF16), uw_ref[t])
         gamps[0] = grad_inv[:, :128]
         for m in range(1, 9):
@@ -314,7 +320,6 @@
         kinds_own, jnp.concatenate([embed, jnp.zeros((16 - species, 128), F32)], axis=0).astype(BF16)
     )
     z1, h1 = update(amps1, h0_own, 0)
-    z1_ref[...] = z1
     h_sec[1, 0:128] = h1
     h_own[...] = h1
 
@@ -329,6 +334,7 @@
     copies = exchange(1, h_parts, lambda side: side[0] == 0)
     h_piece[...] = mm(ohxt[...], h1).astype(BF16)
     copies += exchange(1, h_parts, lambda side: side[0] != 0)
+    z1_ref[...] = slope(z1)
 
     def second_radial(g, carry):
         rad2[:, lanes(g)] = mm(w_t, basis[g])
@@ -362,7 +368,7 @@
         second(p, p == PAIRS - 1)
     z2, h2 = update(amps2, h1.astype(F32), 1)
     out_w = ow_ref[...]
-    back(amps2, z2, out_w, 1)
+    back(amps2, slope(z2), out_w, 1)
 
     def chunk_rows(ref, g):
         at = pl.ds(pl.multiple_of(g * GROUP, GROUP), GROUP)
@@ -448,9 +454,16 @@
         gharm[g] += harmonic_rows(mm(grads.astype(BF16), phi[g]))
         by_kind = mm(grads.T.astype(BF16), hmat[g, 0:80])
         kind = jnp.broadcast_to(spc_d[pl.ds(g, 1), :], (NB, EDGES))
-        by_basis = jnp.where(kind == 0, by_kind[0:NB], 0.0)
-        for k in range(1, species):
-            by_basis += jnp.where(kind == k, by_kind[k * NB : (k + 1) * NB], 0.0)
+        blocks = [by_kind[k * NB : (k + 1) * NB] for k in range(species)]
+        bit = 1
+        while len(blocks) > 1:
+            odd = (kind & bit) != 0
+            blocks = [
+                jnp.where(odd, blocks[k + 1], blocks[k]) if k + 1 < len(blocks) else blocks[k]
+                for k in range(0, len(blocks), 2)
+            ]
+            bit *= 2
+        by_basis = blocks[0]
         gdist[pl.ds(g, 1), :] += distance_row(g, by_basis)
         return carry
 
@@ -593,26 +606,28 @@
         jax.ShapeDtypeStruct((1, ATOMS), F32),
         jax.ShapeDtypeStruct((3, ATOMS), F32),
     )
+    inputs = tuple(pltpu.with_memory_space_constraint(v, pltpu.HBM) for v in inputs)
     results = pl.pallas_call(
         functools.partial(kernel, remote),
         out_shape=shapes,
-        in_specs=[pl.BlockSpec(memory_space=pl.ANY)] * len(inputs),
+        in_specs=[pl.BlockSpec(memory_space=pltpu.HBM)] * len(inputs),
         out_specs=(pl.BlockSpec(memory_space=pltpu.VMEM), pl.BlockSpec(memory_space=pltpu.VMEM)),
         scratch_shapes=[pltpu.VMEM(v.shape, v.dtype) for v in inputs] + scratch,
         compiler_params=pltpu.CompilerParams(
             collective_id=0 if remote else None,
             has_side_effects=remote,
-            vmem_limit_bytes=60 * 1024 * 1024,
+            vmem_limit_bytes=44 * 1024 * 1024,
         ),
     )(*inputs)
     anywhere = pl.BlockSpec(memory_space=pl.ANY)
+    vmem = pl.BlockSpec(memory_space=pltpu.VMEM)
     energy, forces = pl.pallas_call(
         place_outputs,
         out_shape=shapes,
-        in_specs=[anywhere, anywhere],
+        in_specs=[vmem, vmem],
         out_specs=(anywhere, anywhere),
         scratch_shapes=[pltpu.SemaphoreType.DMA((2,))],
-        compiler_params=pltpu.CompilerParams(vmem_limit_bytes=60 * 1024 * 1024),
+        compiler_params=pltpu.CompilerParams(vmem_limit_bytes=1024 * 1024),
     )(*results)
     return energy.reshape(ATOMS), forces
 

time: 49.3 us -> 48.2 us (0.978)
  Pallas kernels: 48.6 us -> 47.5 us
    pallas_call x1, Pallas kernels: 1.18 us -> 0.59 us  [body(): pl.pallas_call(place_outputs, out_shape=shapes, in_specs=[vmem, vmem], ou...]
    pallas_call x1, Pallas kernels: 47.4 us -> 46.9 us  [body(): pl.pallas_call(functools.partial(kernel, remote), out_shape=shapes, in_sp...]
where the time goes in v5:
time: 48.2 us; the launch traced here: 48.1 us
  Pallas kernels  47.5 us (99%)
  between operations  0.64 us (1%)
    pallas_call x1, Pallas kernels, body(): pl.pallas_call(functools.partial(kernel, remote), out_shape=shapes, in_sp...  46.9 us

profile of v5, /device:TPU:1, one launch (start us, length us, event | category | flops | bytes accessed | tf_op | source)
XLA Modules:
  0.0 48.1 jit_solution(18084695280060727337)
XLA Ops:
  0.6 46.9 %shard_map.113 = (f32[1,128]{1,0:T(1,128)S(1)}, f32[3,128]{1,0:T(4,128)S(1)}) custom-call(bf16[3,128]{1,0:T(4,128)(2,1)} %refs_0_.1, s32[1,128]{1,0:T(1,128)} %bitcast.10, s32[48,128]{1,0:T(8,128)} %bitcast.7, s32[1,128]{1,0:T(1,128)} %bitcast.11, s32[2,64]{1,0:T(2,128)} %bitcast.8, s32[2,128]{1,0:T(2,128)} %bitcast.9, bf16[10,128]{1,0:T(8,128)(2,1)} %refs_6_.1, ...), custom_call_target="tpu_custom_call" | custom-call | tf_op jit(solution)/shard_map/pallas_call | solution.py:610
  47.5 0.6 %shard_map.114 = (f32[1,128]{1,0:T(1,128)}, f32[3,128]{1,0:T(4,128)}) custom-call(f32[1,128]{1,0:T(1,128)S(1)} %get-tuple-element.6.energy_in, f32[3,128]{1,0:T(4,128)S(1)} %get-tuple-element.7.forces_in), custom_call_target="tpu_custom_call" | custom-call | tf_op jit(solution)/shard_map/pallas_call | solution.py:624

commit v6 on v5

--- a/solution.py
+++ b/solution.py
@@ -289,7 +289,7 @@
         store_sums(kinds_amps, g, sums_of(g, phi[g], phi_low))
         return carry
 
-    lax.fori_loop(0, CHUNKS, first, 0, unroll=8)
+    lax.fori_loop(0, CHUNKS, first, 0, unroll=16)
     for m in range(9):
         high, low = (v.astype(BF16) for v in split(kinds_amps[m]))
         amps1[m] = mm(high, kind_high) + mm(low, kind_high) + mm(high, kind_low)
@@ -333,7 +333,8 @@
 
     copies = exchange(1, h_parts, lambda side: side[0] == 0)
     h_piece[...] = mm(ohxt[...], h1).astype(BF16)
-    copies += exchange(1, h_parts, lambda side: side[0] != 0)
+    copies += exchange(1, h_parts, lambda side: side[0] != 0 and side[1] != 0)
+    near = exchange(1, h_parts, lambda side: side[1] == 0)
     z1_ref[...] = slope(z1)
 
     def second_radial(g, carry):
@@ -342,16 +343,23 @@
 
     lax.fori_loop(0, CHUNKS, second_radial, 0, unroll=8)
     own_t = h1.astype(F32).T
+    finish(near)
+
+    got_t = h_sec[1, 128:256].astype(F32).T
+    near_t = jnp.concatenate([own_t, got_t], axis=1).astype(BF16)
+
+    def first_section(p, carry):
+        gat2[:, lanes(p, 2)] = mm(near_t, hot[0:256, lanes(p, 2)]).astype(BF16)
+        return carry
+
+    lax.fori_loop(0, PAIRS, first_section, 0, unroll=4)
     finish(copies)
-
-    got_t = h_sec[1, 128:256].astype(F32).T
     low_t = mm(ohyt[0], h_sec[0]).T
     high_t = mm(ohyt[1], h_sec[2]).T
-    h_t = jnp.concatenate([own_t, got_t, low_t, high_t], axis=1).astype(BF16)
+    far_t = jnp.concatenate([low_t, high_t], axis=1).astype(BF16)
 
     def gather(p):
-        gathered = mm(h_t, hot[:, lanes(p, 2)])
-        gat2[:, lanes(p, 2)] = gathered.astype(BF16)
+        gat2[:, lanes(p, 2)] += mm(far_t, hot[256:512, lanes(p, 2)]).astype(BF16)
 
     def second(p, last):
         if not last:
@@ -467,7 +475,7 @@
         gdist[pl.ds(g, 1), :] += distance_row(g, by_basis)
         return carry
 
-    lax.fori_loop(0, CHUNKS, geometry_one, 0, unroll=8)
+    lax.fori_loop(0, CHUNKS, geometry_one, 0, unroll=16)
 
     inv, vx, vy, vz = (vec_d[n] for n in range(2, 6))
     g1, g2, g3, g4, g5, g6, g7, g8 = (SCALE * gharm[:, n, :] for n in range(8))

time: 48.2 us -> 47.2 us (0.979)
  Pallas kernels: 47.5 us -> 46.3 us
    pallas_call x1, Pallas kernels: 46.9 us -> 45.7 us  [body(): pl.pallas_call(functools.partial(kernel, remote), out_shape=shapes, in_sp...]
where the time goes in v6:
time: 47.2 us; the launch traced here: 47 us
  Pallas kernels  46.3 us (98%)
  between operations  0.64 us (1%)
    pallas_call x1, Pallas kernels, body(): pl.pallas_call(functools.partial(kernel, remote), out_shape=shapes, in_sp...  45.7 us

profile of v6, /device:TPU:1, one launch (start us, length us, event | category | flops | bytes accessed | tf_op | source)
XLA Modules:
  0.0 47.0 jit_solution(11904200868605552041)
XLA Ops:
  0.6 45.7 %shard_map.113 = (f32[1,128]{1,0:T(1,128)S(1)}, f32[3,128]{1,0:T(4,128)S(1)}) custom-call(bf16[3,128]{1,0:T(4,128)(2,1)} %refs_0_.1, s32[1,128]{1,0:T(1,128)} %bitcast.10, s32[48,128]{1,0:T(8,128)} %bitcast.7, s32[1,128]{1,0:T(1,128)} %bitcast.11, s32[2,64]{1,0:T(2,128)} %bitcast.8, s32[2,128]{1,0:T(2,128)} %bitcast.9, bf16[10,128]{1,0:T(8,128)(2,1)} %refs_6_.1, ...), custom_call_target="tpu_custom_call" | custom-call | tf_op jit(solution)/shard_map/pallas_call | solution.py:618
  46.4 0.6 %shard_map.114 = (f32[1,128]{1,0:T(1,128)}, f32[3,128]{1,0:T(4,128)}) custom-call(f32[1,128]{1,0:T(1,128)S(1)} %get-tuple-element.6.energy_in, f32[3,128]{1,0:T(4,128)S(1)} %get-tuple-element.7.forces_in), custom_call_target="tpu_custom_call" | custom-call | tf_op jit(solution)/shard_map/pallas_call | solution.py:632

commit v7 on v6

--- a/solution.py
+++ b/solution.py
@@ -258,7 +258,7 @@
         right = [high, low] if high.shape[0] == 128 else [high, fill, low]
         both = nt(hmat[g], jnp.concatenate(right, axis=0))
         n = high.shape[0]
-        return both[:80, :n] + both[:80, 128 : 128 + n] + both[80:, :n]
+        return both[:72, :n] + both[:72, 128 : 128 + n] + both[72:, :n]
 
     def store_sums(ref, g, sums):
         at = pl.ds(pl.multiple_of(g * GROUP, GROUP), GROUP)
@@ -272,8 +272,7 @@
         for m in range(8):
             rows.append(jnp.where(mask, harm_t[m, pl.ds(g, 1), :], 0.0))
             fine.append(jnp.where(mask, harm_t[8 + m, pl.ds(g, 1), :], 0.0))
-        hmat[g, 0:80] = jnp.concatenate(rows + [none], axis=0).astype(BF16)
-        hmat[g, 80:160] = jnp.concatenate(fine + [none], axis=0).astype(BF16)
+        hmat[g] = jnp.concatenate(rows + fine, axis=0).astype(BF16)
         high, low = split(radial_basis(g)[1])
         basis[g] = jnp.concatenate([high, low, high, none], axis=0).astype(BF16)
         kind = jnp.broadcast_to(spc_d[pl.ds(g, 1), :], (16, EDGES)).astype(jnp.int16)
@@ -454,8 +453,9 @@
     grad_h1 += mm(ohx[...], piece.astype(BF16))
     back(amps1, z1_ref[...], grad_h1, 0)
 
+    by_kinds = nt(gamps[...].reshape(9 * ATOMS, WIDTH).astype(BF16), kind_high)
     for m in range(9):
-        kinds_amps[m] = nt(gamps[m].astype(BF16), kind_high)
+        kinds_amps[m] = by_kinds[m * ATOMS : (m + 1) * ATOMS]
 
     def geometry_one(g, carry):
         grads = chunk_rows(kinds_amps, g)
@@ -575,7 +575,7 @@
         pltpu.VMEM((16, CHUNKS, EDGES), F32),
         pltpu.VMEM((EXT, CHUNKS * EDGES), BF16),
         pltpu.VMEM((64, CHUNKS * EDGES), BF16),
-        pltpu.VMEM((CHUNKS, 160, EDGES), BF16),
+        pltpu.VMEM((CHUNKS, 144, EDGES), BF16),
         pltpu.VMEM((CHUNKS, 32, EDGES), BF16),
         pltpu.VMEM((CHUNKS, kinds, EDGES), BF16),
         pltpu.VMEM(whole, F32),

time: 47.2 us -> 47.6 us (level)
  Pallas kernels: 46.3 us -> 46.9 us
    pallas_call x1, Pallas kernels: 45.7 us -> 46.3 us  [body(): pl.pallas_call(functools.partial(kernel, remote), out_shape=shapes, in_sp...]
where the time goes in v7:
time: 47.6 us; the launch traced here: 47.5 us
  Pallas kernels  46.9 us (99%)
  between operations  0.64 us (1%)
    pallas_call x1, Pallas kernels, body(): pl.pallas_call(functools.partial(kernel, remote), out_shape=shapes, in_sp...  46.3 us

profile of v7, /device:TPU:1, one launch (start us, length us, event | category | flops | bytes accessed | tf_op | source)
XLA Modules:
  0.0 47.5 jit_solution(14447578549651103541)
XLA Ops:
  0.6 46.3 %shard_map.113 = (f32[1,128]{1,0:T(1,128)S(1)}, f32[3,128]{1,0:T(4,128)S(1)}) custom-call(bf16[3,128]{1,0:T(4,128)(2,1)} %refs_0_.1, s32[1,128]{1,0:T(1,128)} %bitcast.10, s32[48,128]{1,0:T(8,128)} %bitcast.7, s32[1,128]{1,0:T(1,128)} %bitcast.11, s32[2,64]{1,0:T(2,128)} %bitcast.8, s32[2,128]{1,0:T(2,128)} %bitcast.9, bf16[10,128]{1,0:T(8,128)(2,1)} %refs_6_.1, ...), custom_call_target="tpu_custom_call" | custom-call | tf_op jit(solution)/shard_map/pallas_call | solution.py:618
  46.9 0.6 %shard_map.114 = (f32[1,128]{1,0:T(1,128)}, f32[3,128]{1,0:T(4,128)}) custom-call(f32[1,128]{1,0:T(1,128)S(1)} %get-tuple-element.6.energy_in, f32[3,128]{1,0:T(4,128)S(1)} %get-tuple-element.7.forces_in), custom_call_target="tpu_custom_call" | custom-call | tf_op jit(solution)/shard_map/pallas_call | solution.py:632
